TPU v7x, 512 devices: a whole 4x8x8 slice. The times are simulated.
512 devices in a mesh: head: 8 (over x, core), ctx: 64 (over y, z).
Axes of the slice: x: 4, y: 8, z: 8, core: 2. Of those that a mesh axis runs over, the one named last changes fastest.
Arguments:
- queries: bfloat16 [512, 1024], P(None, 'head'), may hold values from -32 to 32
- keys: bfloat16 [512, 65536], P('head', 'ctx'), may hold values from -6 to 6
- values: bfloat16 [512, 65536], P('head', 'ctx'), may hold values from -6 to 6
- positions: float32 [3, 65536], P(None, 'ctx'), may hold values from 0 to 4
- falloff: float32 [8], P('head'), may hold values from 0.05 to 1
- query_ids: int32 [1024], replicated, may hold values from 0 to 65535
- cotangent: bfloat16 [512, 1024], P(None, 'head'), may hold values from -6 to 6
Outputs:
- attended: bfloat16 [512, 1024], P('head')
- query_grad: float32 [512, 1024], P('head')
- forces: float32 [3, 1024], replicated
All inputs are finite; a program needn't handle non-finite values.
Results may differ from a plain program's by a relative error of at most 0.013.
Values may be sent and summed in bfloat16 or wider, within the bound.
A program may use at most 128 MiB of HBM per device.

v0:
```python
import math

import jax
import jax.numpy as jnp
from jax import lax
from jax.sharding import PartitionSpec as P

HEAD_DIM = 64


def shards(queries, keys, values, positions, falloff, query_ids, cotangent):
    scaling = HEAD_DIM ** (-0.5)
    query_rows, grad_rows = (
        lax.all_to_all(queries, "head", split_axis=0, concat_axis=1, tiled=True),
        lax.all_to_all(cotangent, "head", split_axis=0, concat_axis=1, tiled=True),
    )
    query_count = query_rows.shape[1]
    head_count = query_rows.shape[0] // HEAD_DIM
    key_count = keys.shape[1]
    key_block = math.gcd(key_count, 512)
    block_count = key_count // key_block
    query_heads = query_rows.reshape(head_count, HEAD_DIM, query_count)
    local_index = query_ids - lax.axis_index("ctx") * key_count
    owner_mask = jnp.logical_and(local_index >= 0, local_index < key_count)
    picked = jnp.take(positions, jnp.clip(local_index, 0, key_count - 1), axis=1)
    picked = picked * owner_mask.astype(jnp.float32)[None, :]
    query_place = lax.psum(picked, "ctx")

    def block_parts(index):
        offset = index * key_block
        key_heads = lax.dynamic_slice_in_dim(keys, offset, key_block, 1).reshape(
            head_count, HEAD_DIM, key_block
        )
        value_heads = lax.dynamic_slice_in_dim(values, offset, key_block, 1).reshape(
            head_count, HEAD_DIM, key_block
        )
        place_part = lax.dynamic_slice_in_dim(positions, offset, key_block, 1)
        dots = (
            jnp.einsum("hcq,hck->hqk", query_heads, key_heads, preferred_element_type=jnp.float32)
            * scaling
        )
        dist = jnp.zeros((query_count, key_block), jnp.float32)
        for axis_id in range(3):
            gap = query_place[axis_id][:, None] - place_part[axis_id][None, :]
            dist = dist + gap * gap
        scores = dots - falloff[:, None, None] * dist[None]
        return (scores, key_heads, value_heads, place_part)

    def forward_step(carry, index):
        run_max, run_total, accum = carry
        scores, key_heads, value_heads, place_part = block_parts(index)
        new_max = jnp.maximum(run_max, jnp.max(scores, axis=-1))
        shrink = jnp.exp(run_max - new_max)
        weights = jnp.exp(scores - new_max[..., None])
        accum = accum * shrink[:, None, :] + jnp.einsum(
            "hck,hqk->hcq",
            value_heads,
            weights.astype(jnp.bfloat16),
            preferred_element_type=jnp.float32,
        )
        run_total = run_total * shrink + jnp.sum(weights, axis=-1)
        return ((new_max, run_total, accum), None)

    start = (
        jnp.full((head_count, query_count), -jnp.inf, jnp.float32),
        jnp.zeros((head_count, query_count), jnp.float32),
        jnp.zeros((head_count, HEAD_DIM, query_count), jnp.float32),
    )
    (row_max, row_total, accum), _ = lax.scan(
        forward_step, start, jnp.arange(block_count, dtype=jnp.int32)
    )
    global_max = lax.pmax(row_max, "ctx")
    factor = jnp.exp(row_max - global_max)
    row_total, accum = lax.psum((row_total * factor, accum * factor[:, None, :]), "ctx")
    row_max = global_max
    grad_heads = grad_rows.reshape(head_count, HEAD_DIM, query_count)
    output32 = accum / row_total[:, None, :]
    attended = output32.reshape(head_count * HEAD_DIM, query_count).astype(jnp.bfloat16)
    log_total = row_max + jnp.log(row_total)
    row_delta = jnp.sum(grad_heads.astype(jnp.float32) * output32, axis=1)

    def backward_step(carry, index):
        grad_part, force_part = carry
        scores, key_heads, value_heads, place_part = block_parts(index)
        probs = jnp.exp(scores - log_total[..., None])
        grad_probs = jnp.einsum(
            "hcq,hck->hqk", grad_heads, value_heads, preferred_element_type=jnp.float32
        )
        grad_scores = probs * (grad_probs - row_delta[..., None])
        grad_part = (
            grad_part
            + jnp.einsum(
                "hck,hqk->hcq",
                key_heads,
                grad_scores.astype(jnp.bfloat16),
                preferred_element_type=jnp.float32,
            )
            * scaling
        )
        pull = jnp.sum(2.0 * falloff[:, None, None] * grad_scores, axis=0)
        toward = lax.dot_general(
            place_part, pull, (((1,), (1,)), ((), ())), precision=lax.Precision.HIGHEST
        )
        force_part = force_part - query_place * jnp.sum(pull, axis=-1)[None, :] + toward
        return ((grad_part, force_part), None)

    start = (
        jnp.zeros((head_count, HEAD_DIM, query_count), jnp.float32),
        jnp.zeros((3, query_count), jnp.float32),
    )
    (grad_part, force_part), _ = lax.scan(
        backward_step, start, jnp.arange(block_count, dtype=jnp.int32)
    )
    query_grad, head_force = lax.psum((grad_part, force_part), "ctx")
    forces = lax.psum(head_force, "head")
    return (attended, query_grad.reshape(head_count * HEAD_DIM, query_count), forces)


def solution(mesh):
    return jax.shard_map(
        shards,
        mesh=mesh,
        in_specs=(
            P(None, "head"),
            P("head", "ctx"),
            P("head", "ctx"),
            P(None, "ctx"),
            P("head"),
            P(),
            P(None, "head"),
        ),
        out_specs=(P("head", None), P("head", None), P()),
        check_vma=False,
    )
```

profile of v0, /device:TPU:1, one launch (start us, length us, event | category | flops | bytes accessed | tf_op | source)
XLA Modules:
  0.0 925.2 jit_solution(12605305617123553743)
XLA Ops:
  7.2 10.2 %all-to-all-start = ((bf16[8,64,128]{2,1,0:T(8,128)(2,1)}), bf16[8,64,128]{2,1,0:T(8,128)(2,1)S(1)}, u32[]{:S(2)}, u32[]{:S(2)}) async-start(bf16[8,64,128]{2,1,0:T(8,128)(2,1)} %bitcast.132), calls=%async_computation | async-start | bytes 262144 | tf_op jit(solution)/shard_map/all_to_all | solution.py:14
  17.3 0.7 compare_and_fusion
  18.1 0.7 fusion.35
  18.8 0.9 copy.19
  19.7 2.8 gather_fusion
  22.5 0.3 multiply_bitcast_fusion
  22.9 229.0 %psum.42 = f32[3,1024]{0,1:T(8,128)S(1)} all-reduce(f32[3,1024]{0,1:T(8,128)S(1)} %multiply_bitcast_fusion), channel_id=1, replica_groups=mesh['head'=8,'ctx'=64] {'ctx'}, use_global_device_ids=true, to_apply=%region_0.1 | all-reduce | flops 3072 | bytes 24576 | tf_op jit(solution)/shard_map/psum | solution.py:27
  251.9 0.2 copy.20
  252.1 60.3 %all-to-all-start.1 = ((bf16[8,64,128]{2,1,0:T(8,128)(2,1)}), bf16[8,64,128]{2,1,0:T(8,128)(2,1)S(1)}, u32[]{:S(2)}, u32[]{:S(2)}) async-start(bf16[8,64,128]{2,1,0:T(8,128)(2,1)} %bitcast.6), calls=%async_computation.1 | async-start | bytes 262144 | tf_op jit(solution)/shard_map/all_to_all | solution.py:15
  312.4 0.1 copy.18
  312.5 0.1 reshape.142
  312.6 7.8 while.29
  312.6 0.6 dynamic_slice.63
  313.8 0.1 constant_dynamic-slice_fusion.4
  313.9 1.6 fusion.61
  315.6 0.3 fusion.63
  315.9 0.5 fusion.65
  316.5 0.6 dynamic_slice.63
  317.7 0.1 constant_dynamic-slice_fusion.4
  317.8 1.6 fusion.61
  319.5 0.3 fusion.63
  319.8 0.5 fusion.65
  320.4 110.5 %pmax.7 = f32[1,1024]{1,0:T(1,128)S(1)} all-reduce(f32[1,1024]{1,0:T(1,128)S(1)} %get-tuple-element.188), channel_id=1, replica_groups=mesh['head'=8,'ctx'=64] {'ctx'}, use_global_device_ids=true, to_apply=%region_5.6 | all-reduce | flops 1024 | bytes 8192 | tf_op jit(solution)/shard_map/pmax | solution.py:72
  430.9 0.7 broadcast_multiply_fusion
  431.6 0.0 all-reduce.5.cloned.1.call-start
  432.3 0.1 copy.21
  432.4 0.1 reshape.143
  432.5 112.6 %psum.44 = f32[1,1024]{1,0:T(1,128)S(1)} all-reduce(f32[1,1024]{1,0:T(1,128)S(1)} %get-tuple-element.400), channel_id=1, replica_groups=mesh['head'=8,'ctx'=64] {'ctx'}, use_global_device_ids=true, to_apply=%region_7.8 | all-reduce | flops 1024 | bytes 8192 | tf_op jit(solution)/shard_map/psum | solution.py:74
  545.1 56.5 %all-reduce.3.cloned.1.call-done = f32[1,64,1024]{2,1,0:T(8,128)} async-done(((f32[1,64,1024]{2,1,0:T(8,128)}), f32[1,64,1024]{2,1,0:T(8,128)}) %all-reduce.3.cloned.1.call-update) | async-done | bytes 262160 | tf_op jit(solution)/shard_map/psum | solution.py:74
  601.6 1.7 multiply_reduce_fusion.1
  603.3 10.9 %while.30 = (s32[]{:T(128)}, f32[1,64,1024]{2,1,0:T(8,128)S(1)}, f32[3,1024]{1,0:T(4,128)S(1)}, s32[2]{0:T(128)S(1)}, bf16[64,1024]{1,0:T(8,128)(2,1)S(1)}, /*in...) while((s32[]{:T(128)}, f32[1,64,1024]{2,1,0:T(8,128)S(1)}, ...), condition=%wide.region_11.12_spmd.clone, body=%wide.region_9.11_spmd.clone.sunk | while | flops 229846016 | bytes 11594042 | solution.py:111
  603.3 0.6 dynamic_slice.68
  604.5 0.1 constant_dynamic-slice_fusion.5
  604.6 0.5 fusion.73
  605.1 2.1 multiply_reduce_fusion.3
  607.2 1.2 fusion.75
  608.4 0.3 fusion.74
  608.8 0.6 dynamic_slice.68
  610.0 0.1 constant_dynamic-slice_fusion.5
  610.1 0.5 fusion.73
  610.6 2.1 multiply_reduce_fusion.3
  612.7 1.2 fusion.75
  613.9 0.3 fusion.74
  614.2 0.7 copy-done
  614.9 0.0 all-reduce.5.cloned.1.call-update
  614.9 222.2 %psum.46 = f32[3,1024]{1,0:T(4,128)S(1)} all-reduce(f32[3,1024]{1,0:T(4,128)S(1)} %get-tuple-element.191), channel_id=1, replica_groups=mesh['head'=8,'ctx'=64] {'ctx'}, use_global_device_ids=true, to_apply=%region_13.14 | all-reduce | flops 3072 | bytes 24576 | tf_op jit(solution)/shard_map/psum | solution.py:114
  837.1 79.5 %psum.47 = f32[3,1024]{1,0:T(4,128)} all-reduce(f32[3,1024]{1,0:T(4,128)S(1)} %psum.46), channel_id=1, replica_groups=mesh['head'=8,'ctx'=64] {'head'}, use_global_device_ids=true, to_apply=%region_14.15 | all-reduce | flops 3072 | bytes 24576 | tf_op jit(solution)/shard_map/psum | solution.py:115
  916.7 1.7 copy.47
  (31 shorter events, 0.2 us)
Async XLA Ops:
  7.2 244.9 %all-to-all-start = ((bf16[8,64,128]{2,1,0:T(8,128)(2,1)}), bf16[8,64,128]{2,1,0:T(8,128)(2,1)S(1)}, u32[]{:S(2)}, u32[]{:S(2)}) async-start(bf16[8,64,128]{2,1,0:T(8,128)(2,1)} %bitcast.132), calls=%async_computation | async-start | bytes 262144 | tf_op jit(solution)/shard_map/all_to_all | solution.py:14
  17.3 295.2 %copy-start.1 = (bf16[64,1024]{1,0:T(8,128)(2,1)S(1)}, bf16[64,1024]{1,0:T(8,128)(2,1)}, u32[]{:S(2)}) copy-start(bf16[64,1024]{1,0:T(8,128)(2,1)} %param.12) | copy-start | bytes 393220
  17.3 295.2 %copy-start.2 = (f32[3,1024]{1,0:T(4,128)S(1)}, f32[3,1024]{1,0:T(4,128)}, u32[]{:S(2)}) copy-start(f32[3,1024]{1,0:T(4,128)} %param.14) | copy-start | bytes 36868
  17.3 295.2 %copy-start.3 = (bf16[64,1024]{1,0:T(8,128)(2,1)S(1)}, bf16[64,1024]{1,0:T(8,128)(2,1)}, u32[]{:S(2)}) copy-start(bf16[64,1024]{1,0:T(8,128)(2,1)} %param.13) | copy-start | bytes 393220
  252.1 180.2 %all-to-all-start.1 = ((bf16[8,64,128]{2,1,0:T(8,128)(2,1)}), bf16[8,64,128]{2,1,0:T(8,128)(2,1)S(1)}, u32[]{:S(2)}, u32[]{:S(2)}) async-start(bf16[8,64,128]{2,1,0:T(8,128)(2,1)} %bitcast.6), calls=%async_computation.1 | async-start | bytes 262144 | tf_op jit(solution)/shard_map/all_to_all | solution.py:15
  312.4 289.3 %all-reduce.3.cloned.1.call-start = ((), (), s32[]{:S(2)}) async-start(), calls=%async_computation.2 | async-start | bytes 524288 | tf_op jit(solution)/shard_map/psum | solution.py:74
  431.6 485.0 %all-reduce.5.cloned.1.call-start = ((), (), s32[]{:S(2)}) async-start(), calls=%async_computation.3 | async-start | bytes 524288 | tf_op jit(solution)/shard_map/psum | solution.py:114
  614.2 0.7 copy-start
Sparse Core Ops, SparseCore 0:
  431.7 169.8 all-reduce.2
  615.1 148.4 all-reduce.4
where the time goes:
time: 927 us; the launch traced here: 925 us
  blocking collectives  754 us (81%)
  starting transfers between devices  70.5 us (8%)
  waiting for transfers between devices  56.5 us (6%)
  between operations  14.9 us (2%)
  matrix products  12.4 us (1%)
  local copies, waits for them, and re-layouts  9.34 us (1%)
    psum x1, blocking collectives, shards(): query_place = lax.psum(picked, 'ctx')  229 us
    psum x1, blocking collectives, shards(): query_grad, head_force = lax.psum((grad_part, force_part), 'ctx')  222 us
    psum x1, blocking collectives, shards(): lax.psum((row_total * factor, accum * factor[:, None, :]), 'ctx')  113 us
    pmax x1, blocking collectives, shards(): global_max = lax.pmax(row_max, 'ctx')  110 us
    psum x1, blocking collectives, shards(): forces = lax.psum(head_force, 'head')  79.5 us
    all_to_all x1, starting transfers between devices, shards(): lax.all_to_all(cotangent, 'head', split_axis=0, concat_axis=1, tiled=True)  60.3 us
    psum x1, waiting for transfers between devices, shards(): lax.psum((row_total * factor, accum * factor[:, None, :]), 'ctx')  56.5 us
  transfers between devices with their start and end apart: 4, of which 1 were waited for; matrix products, arithmetic and copies ran while one was open for 1% of the time, Pallas kernels for 0%

commit v1 on v0

v1 whole, which is shorter than its diff:
```python
import functools

import jax
import jax.numpy as jnp
from jax import lax
from jax.experimental import pallas as pl
from jax.experimental.pallas import tpu as pltpu
from jax.sharding import PartitionSpec as P

MESH = pl.DeviceIdType.MESH
HEAD_DIM = 64
SIDE = 8
LANES = 128
CENTER = 2.0
F32 = jnp.float32
BF16 = jnp.bfloat16


def dot(a, b):
    return jnp.dot(a, b, preferred_element_type=F32)


def pieces(x, count):
    out = []
    for _ in range(count):
        part = x.astype(BF16).astype(F32)
        out.append(part)
        x = x - part
    return out


def rows(shape):
    return lax.broadcasted_iota(jnp.int32, shape, 0)


def merge(stats, parts):
    logs = [s[3:4] for s in stats]
    deltas = [s[7:8] for s in stats]
    top = functools.reduce(jnp.maximum, logs)
    weights = [jnp.exp(x - top) for x in logs]
    total = functools.reduce(jnp.add, weights)
    inverse = 1.0 / total
    weights = [w * inverse for w in weights]
    delta = functools.reduce(jnp.add, [w * d for w, d in zip(weights, deltas)])
    shifts = [w * (d - delta) for w, d in zip(weights, deltas)]
    plain = functools.reduce(jnp.add, [w * s for w, s in zip(weights, stats)])
    moved = functools.reduce(
        jnp.add, [t * pltpu.roll(s, 4, 0) for t, s in zip(shifts, stats)]
    )
    at = rows(plain.shape)
    stat = jnp.where(
        at < 3,
        plain + moved,
        jnp.where(at == 3, top + jnp.log(total), jnp.where(at < 7, plain, delta)),
    )
    a = b = c = None
    for i, (w, t) in enumerate(zip(weights, shifts)):
        ai, bi, ci = parts(i)
        ai, bi, ci = w * ai, w * bi + t * ci, w * ci
        a, b, c = (ai, bi, ci) if a is None else (a + ai, b + bi, c + ci)
    return a, b, c, stat


def kernel(
    q_hbm, k_hbm, v_hbm, pos_ref, fall_ref, ids_ref, g_hbm,
    att_ref, qg_ref, f_ref,
    left, kt, vt, xs, qin, gin, qx, pick1, pick2, pick3, s_buf, p_buf, dp_buf,
    part_buf, stat_buf, sb2, rb2, gath, fin, fgath,
    local_sem, send, recv,
):
    h, ctx = lax.axis_index("head"), lax.axis_index("ctx")
    parity = h % 2
    y, z = ctx // SIDE, ctx % SIDE
    m1, m2 = SIDE - (SIDE - 1) * parity, 1 + (SIDE - 1) * parity
    a1 = y + parity * (z - y)
    a2 = z + parity * (y - z)

    def peer1(o):
        b = (a1 + o) % SIDE
        return (h, b * m1 + a2 * m2)

    def peer2(o):
        b = (a2 + o) % SIDE
        return (h, a1 * m1 + b * m2)

    def peerh(o):
        return ((h + o) % SIDE, ctx)

    def peerf(o):
        other = (h + o) % SIDE
        odd = (other + h) % 2
        flipped = z * SIDE + y
        return (other, ctx + odd * (flipped - ctx))

    def copy(phase, o, src, dst, dev):
        return pltpu.make_async_remote_copy(
            src_ref=src, dst_ref=dst, send_sem=send.at[phase, o],
            recv_sem=recv.at[phase, o], device_id=dev, device_id_type=MESH,
        )

    def loop(body):
        def step(o, carry):
            body(o)
            return carry
        lax.fori_loop(1, SIDE, step, 0)

    load_v = pltpu.make_async_copy(v_hbm, left.at[pl.ds(0, 64)], local_sem.at[0])
    load_k = pltpu.make_async_copy(k_hbm, left.at[pl.ds(64, 64)], local_sem.at[1])
    own_rows = pl.ds(pl.multiple_of(h * HEAD_DIM, HEAD_DIM), HEAD_DIM)
    load_q = pltpu.make_async_copy(q_hbm.at[own_rows], qin.at[h], local_sem.at[2])
    load_g = pltpu.make_async_copy(g_hbm.at[own_rows], gin.at[h], local_sem.at[3])
    load_v.start()
    load_k.start()
    load_q.start()
    load_g.start()

    barrier = pltpu.get_barrier_semaphore()

    def greet(o):
        for dev in (peer1(o), peer2(o), peerh(o), peerf(o)):
            pl.semaphore_signal(barrier, inc=1, device_id=dev, device_id_type=MESH)

    loop(greet)

    place = pos_ref[...] - CENTER
    falloff = fall_ref[0]
    xs[0:3, :] = place
    xs[3:4, :] = -falloff * jnp.sum(place * place, axis=0, keepdims=True)
    xs[4:7, :] = place
    xs[7:8, :] = jnp.ones((1, place.shape[1]), F32)
    x1, x2, x3 = pieces(xs[...], 3)
    keys_at = jnp.concatenate([x1, x2, x3, x1], axis=0).astype(BF16)
    left[128:144, :] = jnp.concatenate([x1, x2], axis=0).astype(BF16)
    key_count = place.shape[1]
    local = ids_ref[pl.ds(h, 1), :] - ctx * key_count
    hot = (rows((key_count, LANES)) == local).astype(F32).astype(BF16)
    found = dot(keys_at, hot)
    pick1[a1] = found[0:8] + found[8:16] + found[16:24]

    pl.semaphore_wait(barrier, 4 * (SIDE - 1))

    loop(lambda o: copy(0, o, pick1.at[a1], pick1.at[a1], peer1(o)).start())

    def send_rows(o):
        other, _ = peerh(o)
        part = pl.ds(pl.multiple_of(other * HEAD_DIM, HEAD_DIM), HEAD_DIM)
        copy(1, o, g_hbm.at[part], gin.at[h], peerh(o)).start()
        copy(2, o, q_hbm.at[part], qin.at[h], peerh(o)).start()

    loop(send_rows)

    load_k.wait()
    load_v.wait()
    kt[...] = jnp.concatenate([left[64:128, :], keys_at], axis=0).T
    vt[...] = left[0:64, :].T
    load_q.wait()
    load_g.wait()

    def source(o, me):
        return (me + SIDE - o) % SIDE

    loop(lambda o: copy(0, o, pick1.at[a1], pick1.at[source(o, a1)], peer1(o)).wait_recv())
    pick2[a2] = functools.reduce(jnp.add, [pick1[i] for i in range(SIDE)])
    loop(lambda o: copy(3, o, pick2.at[a2], pick2.at[a2], peer2(o)).start())

    def wait_g(o):
        copy(1, o, gin.at[h], gin.at[source(o, h)], peerh(o)).wait_recv()

    def wait_q(o):
        copy(2, o, qin.at[h], qin.at[source(o, h)], peerh(o)).wait_recv()

    loop(wait_g)

    def chunk(o):
        return (a1 + o) % SIDE

    def grads(t):
        cot = jnp.concatenate([gin[chunk(2 * t + 1)], gin[chunk(2 * t + 2)]], axis=1)
        dp_buf[t] = dot(vt[...], cot)

    def grad_step(t, carry):
        grads(t)
        return carry

    lax.fori_loop(0, 2, grad_step, 0)
    loop(lambda o: copy(3, o, pick2.at[a2], pick2.at[source(o, a2)], peer2(o)).wait_recv())
    pick3[h] = functools.reduce(jnp.add, [pick2[i] for i in range(SIDE)])
    loop(lambda o: copy(4, o, pick3.at[h], pick3.at[h], peerh(o)).start())
    lax.fori_loop(2, 4, grad_step, 0)
    loop(wait_q)
    loop(lambda o: copy(4, o, pick3.at[h], pick3.at[source(o, h)], peerh(o)).wait_recv())

    def build(c, carry):
        spot = pick3[c]
        at = rows(spot.shape)
        side = jnp.where(at < 3, (2.0 * falloff) * spot, jnp.where(at == 3, 1.0, 0.0))
        t1, t2 = pieces(side, 2)
        qx[c, 0:64, :] = qin[c] * jnp.asarray(HEAD_DIM ** -0.5, BF16)
        qx[c, 64:96, :] = jnp.concatenate([t1, t1, t1, t2], axis=0).astype(BF16)
        return carry

    lax.fori_loop(0, SIDE, build, 0)

    blocks = [pl.ds(i * 256, 256) for i in range(key_count // 256)]

    def attend(t, carry):
        chunks = [chunk(2 * t + 1), chunk(2 * t + 2)]
        q = jnp.concatenate([qx[c] for c in chunks], axis=1)
        cot = jnp.concatenate([gin[c] for c in chunks], axis=1).astype(F32)
        top = None
        for part in blocks:
            s = dot(kt[part, :], q)
            s_buf[part, :] = s
            m = jnp.max(s, axis=0, keepdims=True)
            top = m if top is None else jnp.maximum(top, m)
        for part in blocks:
            p = jnp.exp(s_buf[part, :] - top)
            s_buf[part, :] = p
            p_buf[part, :] = p.astype(BF16)
        r = dot(left[...], p_buf[...])
        total = r[135:136]
        inverse = 1.0 / total
        a = r[0:64] * inverse
        c = r[64:128] * inverse
        px = (r[128:136] + r[136:144]) * inverse
        delta = jnp.sum(a * cot, axis=0, keepdims=True)
        for part in blocks:
            w = s_buf[part, :] * (dp_buf[t, part, :] - delta)
            p_buf[part, :] = w.astype(BF16)
        r = dot(left[64:144, :], p_buf[...])
        b = r[0:64] * inverse
        wx = (r[64:72] + r[72:80]) * inverse
        spot = jnp.concatenate([pick3[c] for c in chunks], axis=1)
        at = rows(spot.shape)
        stat = jnp.where(
            at < 3,
            wx - spot * wx[7:8],
            jnp.where(
                at == 3,
                top + jnp.log(total),
                jnp.where(at < 7, px - spot * px[7:8], delta),
            ),
        )
        for i in range(2):
            o = (2 * t + 1 + i) % SIDE
            slot = jnp.where(o == 0, a1, SIDE + o)
            lanes = slice(i * LANES, (i + 1) * LANES)
            part_buf[slot, 0:64, :] = a[:, lanes].astype(BF16)
            part_buf[slot, 64:128, :] = b[:, lanes].astype(BF16)
            part_buf[slot, 128:192, :] = c[:, lanes].astype(BF16)
            stat_buf[slot] = stat[:, lanes]

            @pl.when(o != 0)
            def _():
                copy(5, o, part_buf.at[slot], part_buf.at[a1], peer1(o)).start()
                copy(6, o, stat_buf.at[slot], stat_buf.at[a1], peer1(o)).start()

        return carry

    lax.fori_loop(0, SIDE // 2, attend, 0)

    def wait_parts(o):
        copy(5, o, part_buf.at[SIDE + o], part_buf.at[source(o, a1)], peer1(o)).wait_recv()
        copy(6, o, stat_buf.at[SIDE + o], stat_buf.at[source(o, a1)], peer1(o)).wait_recv()

    loop(wait_parts)

    def parts1(i):
        x = part_buf[i].astype(F32)
        return x[0:64], x[64:128], x[128:192]

    a, b, c, stat = merge([stat_buf[i] for i in range(SIDE)], parts1)
    for j in range(SIDE):
        part = slice(8 * j, 8 * j + 8)
        sb2[j, 0:8, :] = a[part]
        sb2[j, 8:16, :] = b[part]
        sb2[j, 16:24, :] = c[part]
        sb2[j, 24:32, :] = stat
    rb2[a2] = sb2[a2]

    def send_second(o):
        copy(7, o, sb2.at[(a2 + o) % SIDE], rb2.at[a2], peer2(o)).start()

    loop(send_second)
    loop(lambda o: copy(7, o, sb2.at[0], rb2.at[source(o, a2)], peer2(o)).wait_recv())

    def parts2(i):
        x = rb2[i]
        return x[0:8], x[8:16], x[16:24]

    a, b, c, stat = merge([rb2[i, 24:32, :] for i in range(SIDE)], parts2)
    gath[a1, a2] = jnp.concatenate([a, b * HEAD_DIM ** -0.5], axis=0).astype(BF16)
    fin[h] = (2.0 * falloff) * stat
    loop(lambda o: copy(8, o, gath.at[a1, a2], gath.at[a1, a2], peer2(o)).start())
    loop(lambda o: copy(9, o, fin.at[h], fin.at[h], peerf(o)).start())
    loop(lambda o: copy(8, o, gath.at[a1, a2], gath.at[a1, source(o, a2)], peer2(o)).wait_recv())
    loop(lambda o: copy(10, o, gath.at[a1], gath.at[a1], peer1(o)).start())
    loop(lambda o: copy(9, o, fin.at[h], fin.at[source(o, h)], peerf(o)).wait_recv())
    fgath[a1] = functools.reduce(jnp.add, [fin[i] for i in range(SIDE)])
    loop(lambda o: copy(11, o, fgath.at[a1], fgath.at[a1], peer1(o)).start())

    loop(lambda o: copy(10, o, gath.at[a1], gath.at[source(o, a1)], peer1(o)).wait_recv())
    for i in range(SIDE):
        lanes = slice(i * LANES, (i + 1) * LANES)
        for j in range(0, SIDE, 2):
            lo, hi = gath[i, j].astype(F32), gath[i, j + 1].astype(F32)
            att_ref[8 * j:8 * j + 16, lanes] = jnp.concatenate([lo[0:8], hi[0:8]], axis=0).astype(BF16)
            qg_ref[8 * j:8 * j + 8, lanes] = lo[8:16]
            qg_ref[8 * j + 8:8 * j + 16, lanes] = hi[8:16]
    loop(lambda o: copy(11, o, fgath.at[a1], fgath.at[source(o, a1)], peer1(o)).wait_recv())
    for i in range(SIDE):
        f_ref[:, i * LANES:(i + 1) * LANES] = fgath[i, 0:3, :]

    def drain(o):
        copy(0, o, pick1.at[a1], pick1.at[a1], peer1(o)).wait_send()
        copy(1, o, gin.at[h], gin.at[h], peerh(o)).wait_send()
        copy(2, o, qin.at[h], qin.at[h], peerh(o)).wait_send()
        copy(3, o, pick2.at[a2], pick2.at[a2], peer2(o)).wait_send()
        copy(4, o, pick3.at[h], pick3.at[h], peerh(o)).wait_send()
        copy(5, o, part_buf.at[SIDE + o], part_buf.at[a1], peer1(o)).wait_send()
        copy(6, o, stat_buf.at[SIDE + o], stat_buf.at[a1], peer1(o)).wait_send()
        copy(7, o, sb2.at[0], rb2.at[a2], peer2(o)).wait_send()
        copy(8, o, gath.at[a1, a2], gath.at[a1, a2], peer2(o)).wait_send()
        copy(9, o, fin.at[h], fin.at[h], peerf(o)).wait_send()
        copy(10, o, gath.at[a1], gath.at[a1], peer1(o)).wait_send()
        copy(11, o, fgath.at[a1], fgath.at[a1], peer1(o)).wait_send()

    loop(drain)


def shards(queries, keys, values, positions, falloff, query_ids, cotangent):
    nk = keys.shape[1]
    nq = query_ids.shape[0]
    ids = query_ids.reshape(SIDE, LANES)
    vmem = pl.BlockSpec(memory_space=pltpu.VMEM)
    smem = pl.BlockSpec(memory_space=pltpu.SMEM)
    any_ = pl.BlockSpec(memory_space=pl.ANY)
    return pl.pallas_call(
        kernel,
        out_shape=(
            jax.ShapeDtypeStruct((HEAD_DIM, nq), BF16),
            jax.ShapeDtypeStruct((HEAD_DIM, nq), F32),
            jax.ShapeDtypeStruct((3, nq), F32),
        ),
        in_specs=[any_, any_, any_, vmem, smem, vmem, any_],
        out_specs=(vmem, vmem, vmem),
        scratch_shapes=[
            pltpu.VMEM((144, nk), BF16),
            pltpu.VMEM((nk, 96), BF16),
            pltpu.VMEM((nk, 64), BF16),
            pltpu.VMEM((8, nk), F32),
            pltpu.VMEM((SIDE, HEAD_DIM, LANES), BF16),
            pltpu.VMEM((SIDE, HEAD_DIM, LANES), BF16),
            pltpu.VMEM((SIDE, 96, LANES), BF16),
            pltpu.VMEM((SIDE, 8, LANES), F32),
            pltpu.VMEM((SIDE, 8, LANES), F32),
            pltpu.VMEM((SIDE, 8, LANES), F32),
            pltpu.VMEM((nk, 2 * LANES), F32),
            pltpu.VMEM((nk, 2 * LANES), BF16),
            pltpu.VMEM((SIDE // 2, nk, 2 * LANES), F32),
            pltpu.VMEM((2 * SIDE, 192, LANES), BF16),
            pltpu.VMEM((2 * SIDE, 8, LANES), F32),
            pltpu.VMEM((SIDE, 32, LANES), F32),
            pltpu.VMEM((SIDE, 32, LANES), F32),
            pltpu.VMEM((SIDE, SIDE, 16, LANES), BF16),
            pltpu.VMEM((SIDE, 8, LANES), F32),
            pltpu.VMEM((SIDE, 8, LANES), F32),
            pltpu.SemaphoreType.DMA((4,)),
            pltpu.SemaphoreType.DMA((12, SIDE)),
            pltpu.SemaphoreType.DMA((12, SIDE)),
        ],
        compiler_params=pltpu.CompilerParams(
            collective_id=0, has_side_effects=True, vmem_limit_bytes=40 * 1024 * 1024
        ),
    )(queries, keys, values, positions, falloff, ids, cotangent)


def solution(mesh):
    return jax.shard_map(
        shards,
        mesh=mesh,
        in_specs=(
            P(None, "head"),
            P("head", "ctx"),
            P("head", "ctx"),
            P(None, "ctx"),
            P("head"),
            P(),
            P(None, "head"),
        ),
        out_specs=(P("head", None), P("head", None), P()),
        check_vma=False,
    )
```

time: 927 us -> 67.5 us (0.07)
  blocking collectives: 754 us -> 0 us
  starting transfers between devices: 70.5 us -> 0 us
  Pallas kernels: 0 us -> 58.9 us
  waiting for transfers between devices: 56.5 us -> 0 us
  between operations: 14.9 us -> 1.3 us
  matrix products: 12.4 us -> 0 us
    psum x4 -> x0, blocking collectives: 643 us -> none  [the longest x1 229 us: shards(): query_place = lax.psum(picked, 'ctx')]
    pmax x1 -> x0, blocking collectives: 110 us -> none  [shards(): global_max = lax.pmax(row_max, 'ctx')]
    all_to_all x2 -> x0, starting transfers between devices: 70.4 us -> none  [the longest x1 60.3 us: shards(): lax.all_to_all(cotangent, 'head', split_axis=0, concat_axis=1, tiled=True)]
    pallas_call x0 -> x1, Pallas kernels: none -> 58.9 us  [shards(): pl.pallas_call(kernel, out_shape=(jax.ShapeDtypeStruct((HEAD_DIM, nq), BF...]
    psum x2 -> x0, waiting for transfers between devices: 56.5 us -> none  [the longest x1 56.5 us: shards(): lax.psum((row_total * factor, accum * factor[:, None, :]), 'ctx')]
    dot_general x12 -> x0, matrix products: 12.4 us -> none  [the longest x2 4.26 us: backward_step(): jnp.einsum('hcq,hck->hqk', grad_heads, value_heads, preferred_element_typ...]
  transfers between devices with their start and end apart: 4 -> 0, of which waited for: 1 -> 0; matrix products, arithmetic and copies ran while one was open for 1% -> 0% of each run, Pallas kernels for 0% -> 0%
where the time goes in v1:
time: 67.5 us; the launch traced here: 67.2 us
  Pallas kernels  58.9 us (87%)
  local copies, waits for them, and re-layouts  6.98 us (10%)
  between operations  1.3 us (2%)
    pallas_call x1, Pallas kernels, shards(): pl.pallas_call(kernel, out_shape=(jax.ShapeDtypeStruct((HEAD_DIM, nq), BF...  58.9 us
    unnamed x15, local copies, waits for them, and re-layouts  6.98 us

profile of v1, /device:TPU:1, one launch (start us, length us, event | category | flops | bytes accessed | tf_op | source)
XLA Modules:
  0.0 67.2 jit_solution(13635610758158810192)
XLA Ops:
  1.3 0.0 copy-start
  1.3 0.9 %copy-done = bf16[512,128]{1,0:T(8,128)(2,1)S(1)} copy-done((bf16[512,128]{1,0:T(8,128)(2,1)S(1)}, bf16[512,128]{1,0:T(8,128)(2,1)}, u32[]{:S(2)}) %copy-start) | copy-done | bytes 131096
  2.2 0.0 copy-start.1
  2.2 0.9 %copy-done.1 = bf16[64,1024]{1,0:T(8,128)(2,1)S(1)} copy-done((bf16[64,1024]{1,0:T(8,128)(2,1)S(1)}, bf16[64,1024]{1,0:T(8,128)(2,1)}, u32[]{:S(2)}) %copy-start.1) | copy-done | bytes 131096
  3.1 0.0 copy-start.2
  3.1 0.9 %copy-done.2 = bf16[64,1024]{1,0:T(8,128)(2,1)S(1)} copy-done((bf16[64,1024]{1,0:T(8,128)(2,1)S(1)}, bf16[64,1024]{1,0:T(8,128)(2,1)}, u32[]{:S(2)}) %copy-start.2) | copy-done | bytes 131096
  4.0 0.0 copy-start.3
  4.0 0.9 %copy-done.3 = bf16[512,128]{1,0:T(8,128)(2,1)S(1)} copy-done((bf16[512,128]{1,0:T(8,128)(2,1)S(1)}, bf16[512,128]{1,0:T(8,128)(2,1)}, u32[]{:S(2)}) %copy-start.3) | copy-done | bytes 131096
  4.9 0.0 copy-start.4
  4.9 0.7 %copy-done.4 = f32[3,1024]{1,0:T(4,128)S(1)} copy-done((f32[3,1024]{1,0:T(4,128)S(1)}, f32[3,1024]{1,0:T(4,128)}, u32[]{:S(2)}) %copy-start.4) | copy-done | bytes 12312
  5.6 0.0 copy-start.5
  5.6 0.7 %copy-done.5 = s32[1024]{0:T(1024)S(1)} copy-done((s32[1024]{0:T(1024)S(1)}, s32[1024]{0:T(1024)}, u32[]{:S(2)}) %copy-start.5) | copy-done | bytes 4120
  6.3 58.9 %shard_map.94 = (bf16[64,1024]{1,0:T(8,128)(2,1)S(1)}, f32[64,1024]{1,0:T(8,128)S(1)}, f32[3,1024]{1,0:T(4,128)S(1)}) custom-call(bf16[512,128]{1,0:T(8,128)(2,1)S(1)} %copy-done, bf16[64,1024]{1,0:T(8,128)(2,1)S(1)} %copy-done.1, bf16[64,1024]{1,0:T(8,128)(2,1)S(1)} %copy-done.2, f32[3,1024]{1,0:T(4,128)S(1)} %copy-done.4, f32[1]{0:T(128)S(6)} %copy.13.fall_ref, ...), custom_call_target="tpu_custom_call" | custom-call | tf_op jit(solution)/shard_map/pallas_call | solution.py:338
  65.2 0.7 copy.14
  65.9 0.7 %copy.15 = f32[64,1024]{1,0:T(8,128)} copy(f32[64,1024]{1,0:T(8,128)S(1)} %get-tuple-element.7) | data formatting | bytes 524288
  66.6 0.6 copy.16
Async XLA Ops:
  1.3 0.9 %copy-start = (bf16[512,128]{1,0:T(8,128)(2,1)S(1)}, bf16[512,128]{1,0:T(8,128)(2,1)}, u32[]{:S(2)}) copy-start(bf16[512,128]{1,0:T(8,128)(2,1)} %q_hbm.1) | copy-start | bytes 393220
  2.2 0.9 %copy-start.1 = (bf16[64,1024]{1,0:T(8,128)(2,1)S(1)}, bf16[64,1024]{1,0:T(8,128)(2,1)}, u32[]{:S(2)}) copy-start(bf16[64,1024]{1,0:T(8,128)(2,1)} %k_hbm.1) | copy-start | bytes 393220
  3.1 0.9 %copy-start.2 = (bf16[64,1024]{1,0:T(8,128)(2,1)S(1)}, bf16[64,1024]{1,0:T(8,128)(2,1)}, u32[]{:S(2)}) copy-start(bf16[64,1024]{1,0:T(8,128)(2,1)} %v_hbm.1) | copy-start | bytes 393220
  4.0 0.9 %copy-start.3 = (bf16[512,128]{1,0:T(8,128)(2,1)S(1)}, bf16[512,128]{1,0:T(8,128)(2,1)}, u32[]{:S(2)}) copy-start(bf16[512,128]{1,0:T(8,128)(2,1)} %g_hbm.1) | copy-start | bytes 393220
  4.9 0.7 %copy-start.4 = (f32[3,1024]{1,0:T(4,128)S(1)}, f32[3,1024]{1,0:T(4,128)}, u32[]{:S(2)}) copy-start(f32[3,1024]{1,0:T(4,128)} %pos_ref.1) | copy-start | bytes 36868
  5.6 0.7 %copy-start.5 = (s32[1024]{0:T(1024)S(1)}, s32[1024]{0:T(1024)}, u32[]{:S(2)}) copy-start(s32[1024]{0:T(1024)} %param.12) | copy-start | bytes 12292

commit v2 on v1

v2 whole, which is shorter than its diff:
```python
import functools

import jax
import jax.numpy as jnp
from jax import lax
from jax.experimental import pallas as pl
from jax.experimental.pallas import tpu as pltpu
from jax.sharding import PartitionSpec as P

MESH = pl.DeviceIdType.MESH
HEAD_DIM = 64
SIDE = 8
LANES = 128
CENTER = 2.0
F32 = jnp.float32
BF16 = jnp.bfloat16


def dot(a, b):
    return jnp.dot(a, b, preferred_element_type=F32)


def pieces(x, count):
    out = []
    for _ in range(count):
        part = x.astype(BF16).astype(F32)
        out.append(part)
        x = x - part
    return out


def rows(shape):
    return lax.broadcasted_iota(jnp.int32, shape, 0)


def merge(stats, parts):
    logs = [s[3:4] for s in stats]
    deltas = [s[7:8] for s in stats]
    top = functools.reduce(jnp.maximum, logs)
    weights = [jnp.exp(x - top) for x in logs]
    total = functools.reduce(jnp.add, weights)
    inverse = 1.0 / total
    weights = [w * inverse for w in weights]
    delta = functools.reduce(jnp.add, [w * d for w, d in zip(weights, deltas)])
    shifts = [w * (d - delta) for w, d in zip(weights, deltas)]
    plain = functools.reduce(jnp.add, [w * s for w, s in zip(weights, stats)])
    moved = functools.reduce(
        jnp.add, [t * pltpu.roll(s, 4, 0) for t, s in zip(shifts, stats)]
    )
    at = rows(plain.shape)
    stat = jnp.where(
        at < 3,
        plain + moved,
        jnp.where(at == 3, top + jnp.log(total), jnp.where(at < 7, plain, delta)),
    )
    a = b = c = None
    for i, (w, t) in enumerate(zip(weights, shifts)):
        ai, bi, ci = parts(i)
        ai, bi, ci = w * ai, w * bi + t * ci, w * ci
        a, b, c = (ai, bi, ci) if a is None else (a + ai, b + bi, c + ci)
    return a, b, c, stat


def kernel(
    q_hbm, k_hbm, v_hbm, pos_hbm, fall_hbm, ids_hbm, g_hbm,
    att_ref, qg_ref, f_ref,
    pos, fall, ids, left, kt, vt, xs, qin, gin, qx, pick1, pick2, pick3, s_buf, p_buf,
    dp_buf, part_buf, stat_buf, sb2, rb2, gath, fin, fgath,
    local_sem, send, recv,
):
    h, ctx = lax.axis_index("head"), lax.axis_index("ctx")
    parity = h % 2
    mate = h + 1 - 2 * parity
    y, z = ctx // SIDE, ctx % SIDE
    m1, m2 = SIDE - (SIDE - 1) * parity, 1 + (SIDE - 1) * parity
    a1 = y + parity * (z - y)
    a2 = z + parity * (y - z)

    def on1(o):
        return ((a1 + o) % SIDE) * m1 + a2 * m2

    def on2(o):
        return a1 * m1 + ((a2 + o) % SIDE) * m2

    def far(k):
        return (SIDE // 2 + (1 - 2 * (k % 2)) * ((k + 1) // 2)) % SIDE

    def copy(phase, src, dst, dev):
        return pltpu.make_async_remote_copy(
            src_ref=src, dst_ref=dst, send_sem=send.at[phase],
            recv_sem=recv.at[phase], device_id=dev, device_id_type=MESH,
        )

    def loop(count, body):
        def step(o, carry):
            body(o)
            return carry
        lax.fori_loop(0, count, step, 0)

    def arrived(phase, ref):
        copy(phase, ref, ref, (h, ctx)).wait_recv()

    def sent(phase, ref):
        copy(phase, ref, ref, (h, ctx)).wait_send()

    def seven(ref):
        return ref.at[pl.ds(0, SIDE - 1)]

    own_rows = pl.ds(pl.multiple_of(h * HEAD_DIM, HEAD_DIM), HEAD_DIM)
    loads = [
        pltpu.make_async_copy(src, dst, local_sem.at[i])
        for i, (src, dst) in enumerate([
            (pos_hbm, pos), (fall_hbm, fall), (ids_hbm, ids),
            (k_hbm, left.at[pl.ds(64, 64)]), (v_hbm, left.at[pl.ds(0, 64)]),
            (g_hbm.at[own_rows], gin.at[h]), (q_hbm.at[own_rows], qin.at[h]),
        ])
    ]
    for load in loads[:3]:
        load.start()

    barrier = pltpu.get_barrier_semaphore()

    def greet(head, at):
        pl.semaphore_signal(barrier, inc=1, device_id=(head, at), device_id_type=MESH)

    def greet_seven(k):
        o = far(k)
        greet(h, on1(o))
        greet(h, on2(o))
        greet((h + o) % SIDE, ctx)

    loop(SIDE - 1, greet_seven)
    loop(SIDE, lambda k: greet(mate, on1(far(k))))

    for load in loads[3:]:
        load.start()
    for load in loads[:3]:
        load.wait()
    place = pos[...] - CENTER
    key_count = place.shape[1]
    falloff = fall[...]
    xs[0:3, :] = place
    xs[3:4, :] = -falloff * jnp.sum(place * place, axis=0, keepdims=True)
    xs[4:7, :] = place
    xs[7:8, :] = jnp.ones((1, key_count), F32)
    x1, x2, x3 = pieces(xs[...], 3)
    keys_at = jnp.concatenate([x1, x2, x3, x1], axis=0).astype(BF16)
    for half in range(2):
        tiles = []
        for i in range(2):
            local = ids[pl.ds(4 * parity + 2 * half + i, 1), :] - ctx * key_count
            hot = (rows((key_count, LANES)) == local).astype(F32).astype(BF16)
            found = dot(keys_at[0:24], hot)
            tiles.append(found[0:8] + found[8:16] + found[16:24])
        pick1[a1, half] = jnp.where(rows(tiles[0].shape) < 4, tiles[0], tiles[1])
    pl.semaphore_wait(barrier, 3 * (SIDE - 1) + SIDE)
    loop(SIDE - 1, lambda k: copy(0, pick1.at[a1], pick1.at[a1], (h, on1(far(k)))).start())

    def send_rows(ref_hbm, ref, phase):
        def body(k):
            other = (h + far(k)) % SIDE
            part = pl.ds(pl.multiple_of(other * HEAD_DIM, HEAD_DIM), HEAD_DIM)
            copy(phase, ref_hbm.at[part], ref.at[h], (other, ctx)).start()
        loop(SIDE - 1, body)

    send_rows(g_hbm, gin, 1)
    send_rows(q_hbm, qin, 2)
    for load in loads[3:]:
        load.wait()
    left[128:144, :] = jnp.concatenate([x1, x2], axis=0).astype(BF16)
    kt[...] = jnp.concatenate([left[64:128, :], keys_at], axis=0).T
    vt[...] = left[0:64, :].T
    arrived(0, seven(pick1))
    pick2[SIDE * parity + a2] = functools.reduce(jnp.add, [pick1[i] for i in range(SIDE)])
    mine = pick2.at[SIDE * parity + a2]
    loop(SIDE - 1, lambda k: copy(3, mine, mine, (h, on2(far(k)))).start())
    loop(SIDE, lambda k: copy(3, mine, mine, (mate, on2(far(k)))).start())
    arrived(1, seven(gin))

    def chunks(t):
        return [(a1 + SIDE // 2 - t) % SIDE, (a1 + SIDE // 2 + 1 + t) % SIDE]

    def grads(t):
        cot = jnp.concatenate([gin[c] for c in chunks(t)], axis=1)
        dp_buf[t] = dot(vt[...], cot)

    loop(SIDE // 2, grads)
    arrived(2, seven(qin))
    arrived(3, pick2.at[pl.ds(0, 2 * SIDE - 1)])
    for p in range(2):
        pairs = functools.reduce(jnp.add, [pick2[SIDE * p + i] for i in range(SIDE)])
        for half in range(2):
            pair = pairs[half]
            low = rows(pair.shape) < 4
            swapped = pltpu.roll(pair, 4, 0)
            pick3[4 * p + 2 * half] = jnp.where(low, pair, swapped)
            pick3[4 * p + 2 * half + 1] = jnp.where(low, swapped, pair)

    def build(c):
        spot = pick3[c]
        at = rows(spot.shape)
        side = jnp.where(at < 3, (2.0 * falloff) * spot, jnp.where(at == 3, 1.0, 0.0))
        t1, t2 = pieces(side, 2)
        qx[c, 0:64, :] = qin[c] * jnp.asarray(HEAD_DIM ** -0.5, BF16)
        qx[c, 64:96, :] = jnp.concatenate([t1, t1, t1, t2], axis=0).astype(BF16)

    loop(SIDE, build)

    blocks = [pl.ds(i * 256, 256) for i in range(key_count // 256)]

    def attend(t):
        mine = chunks(t)
        q = jnp.concatenate([qx[c] for c in mine], axis=1)
        cot = jnp.concatenate([gin[c] for c in mine], axis=1).astype(F32)
        top = None
        for part in blocks:
            s = dot(kt[part, :], q)
            s_buf[part, :] = s
            m = jnp.max(s, axis=0, keepdims=True)
            top = m if top is None else jnp.maximum(top, m)
        for part in blocks:
            p = jnp.exp(s_buf[part, :] - top)
            s_buf[part, :] = p
            p_buf[part, :] = p.astype(BF16)
        r = dot(left[...], p_buf[...])
        total = r[135:136]
        inverse = 1.0 / total
        a = r[0:64] * inverse
        c = r[64:128] * inverse
        px = (r[128:136] + r[136:144]) * inverse
        delta = jnp.sum(a * cot, axis=0, keepdims=True)
        for part in blocks:
            w = s_buf[part, :] * (dp_buf[t, part, :] - delta)
            p_buf[part, :] = w.astype(BF16)
        r = dot(left[64:144, :], p_buf[...])
        b = r[0:64] * inverse
        wx = (r[64:72] + r[72:80]) * inverse
        spot = jnp.concatenate([pick3[c] for c in mine], axis=1)
        at = rows(spot.shape)
        stat = jnp.where(
            at < 3,
            wx - spot * wx[7:8],
            jnp.where(
                at == 3,
                top + jnp.log(total),
                jnp.where(at < 7, px - spot * px[7:8], delta),
            ),
        )
        for i in range(2):
            o = (mine[i] + SIDE - a1) % SIDE
            slot = jnp.where(o == 0, a1, SIDE + o)
            lanes = slice(i * LANES, (i + 1) * LANES)
            part_buf[slot, 0:64, :] = a[:, lanes].astype(BF16)
            part_buf[slot, 64:128, :] = b[:, lanes].astype(BF16)
            part_buf[slot, 128:192, :] = c[:, lanes].astype(BF16)
            stat_buf[slot] = stat[:, lanes]

            @pl.when(o != 0)
            def _():
                copy(4, part_buf.at[slot], part_buf.at[a1], (h, on1(o))).start()
                copy(5, stat_buf.at[slot], stat_buf.at[a1], (h, on1(o))).start()

    loop(SIDE // 2, attend)
    arrived(5, seven(stat_buf))
    arrived(4, seven(part_buf))
    def parts1(i):
        x = part_buf[i].astype(F32)
        return x[0:64], x[64:128], x[128:192]

    a, b, c, stat = merge([stat_buf[i] for i in range(SIDE)], parts1)
    for j in range(SIDE):
        part = slice(8 * j, 8 * j + 8)
        sb2[j, 0:8, :] = a[part]
        sb2[j, 8:16, :] = b[part]
        sb2[j, 16:24, :] = c[part]
        sb2[j, 24:32, :] = stat
    def send_second(k):
        o = far(k)
        copy(6, sb2.at[(a2 + o) % SIDE], rb2.at[a2], (h, on2(o))).start()

    loop(SIDE - 1, send_second)
    rb2[a2] = sb2[a2]
    arrived(6, seven(rb2))
    def parts2(i):
        x = rb2[i]
        return x[0:8], x[8:16], x[16:24]

    a, b, c, stat = merge([rb2[i, 24:32, :] for i in range(SIDE)], parts2)
    fin[h // 2] = (2.0 * falloff) * stat
    tile = SIDE * a1 + a2
    gath[tile] = jnp.concatenate([a, b * HEAD_DIM ** -0.5], axis=0).astype(BF16)
    def send_force(k):
        other = (h + 2 + 2 * k) % SIDE
        copy(7, fin.at[h // 2], fin.at[h // 2], (other, ctx)).start()

    loop(3, send_force)

    def send_tile(k1, k2):
        at = ((a1 + far(k1)) % SIDE) * m1 + ((a2 + far(k2)) % SIDE) * m2
        copy(8, gath.at[tile], gath.at[tile], (h, at)).start()

    loop(SIDE * (SIDE - 1), lambda k: send_tile(k // SIDE, k % SIDE))
    loop(SIDE - 1, lambda k: send_tile(SIDE - 1, k))
    arrived(7, fin.at[pl.ds(0, 3)])
    fgath[SIDE * parity + a1] = functools.reduce(jnp.add, [fin[i] for i in range(4)])
    ours = fgath.at[SIDE * parity + a1]
    loop(SIDE - 1, lambda k: copy(9, ours, ours, (h, on1(far(k)))).start())
    loop(SIDE, lambda k: copy(9, ours, ours, (mate, on1(far(k)))).start())
    arrived(8, gath.at[pl.ds(0, SIDE * SIDE - 1)])
    for i in range(SIDE):
        lanes = slice(i * LANES, (i + 1) * LANES)
        for j in range(0, SIDE, 2):
            lo, hi = gath[SIDE * i + j].astype(F32), gath[SIDE * i + j + 1].astype(F32)
            att_ref[8 * j:8 * j + 16, lanes] = jnp.concatenate([lo[0:8], hi[0:8]], axis=0).astype(BF16)
            qg_ref[8 * j:8 * j + 8, lanes] = lo[8:16]
            qg_ref[8 * j + 8:8 * j + 16, lanes] = hi[8:16]
    arrived(9, fgath.at[pl.ds(0, 2 * SIDE - 1)])
    for i in range(SIDE):
        f_ref[:, i * LANES:(i + 1) * LANES] = fgath[i, 0:3, :] + fgath[SIDE + i, 0:3, :]
    sent(0, seven(pick1))
    sent(1, seven(gin))
    sent(2, seven(qin))
    sent(3, pick2.at[pl.ds(0, 2 * SIDE - 1)])
    sent(4, seven(part_buf))
    sent(5, seven(stat_buf))
    sent(6, seven(rb2))
    sent(7, fin.at[pl.ds(0, 3)])
    sent(8, gath.at[pl.ds(0, SIDE * SIDE - 1)])
    sent(9, fgath.at[pl.ds(0, 2 * SIDE - 1)])


def shards(queries, keys, values, positions, falloff, query_ids, cotangent):
    nk = keys.shape[1]
    nq = query_ids.shape[0]
    ids = query_ids.reshape(SIDE, LANES)
    vmem = pl.BlockSpec(memory_space=pltpu.VMEM)
    any_ = pl.BlockSpec(memory_space=pl.ANY)
    return pl.pallas_call(
        kernel,
        out_shape=(
            jax.ShapeDtypeStruct((HEAD_DIM, nq), BF16),
            jax.ShapeDtypeStruct((HEAD_DIM, nq), F32),
            jax.ShapeDtypeStruct((3, nq), F32),
        ),
        in_specs=[any_] * 7,
        out_specs=(vmem, vmem, vmem),
        scratch_shapes=[
            pltpu.VMEM((3, nk), F32),
            pltpu.VMEM((1, 1), F32),
            pltpu.VMEM((SIDE, LANES), jnp.int32),
            pltpu.VMEM((144, nk), BF16),
            pltpu.VMEM((nk, 96), BF16),
            pltpu.VMEM((nk, 64), BF16),
            pltpu.VMEM((8, nk), F32),
            pltpu.VMEM((SIDE, HEAD_DIM, LANES), BF16),
            pltpu.VMEM((SIDE, HEAD_DIM, LANES), BF16),
            pltpu.VMEM((SIDE, 96, LANES), BF16),
            pltpu.VMEM((SIDE, 2, 8, LANES), F32),
            pltpu.VMEM((2 * SIDE, 2, 8, LANES), F32),
            pltpu.VMEM((SIDE, 8, LANES), F32),
            pltpu.VMEM((nk, 2 * LANES), F32),
            pltpu.VMEM((nk, 2 * LANES), BF16),
            pltpu.VMEM((SIDE // 2, nk, 2 * LANES), F32),
            pltpu.VMEM((2 * SIDE, 192, LANES), BF16),
            pltpu.VMEM((2 * SIDE, 8, LANES), F32),
            pltpu.VMEM((SIDE, 32, LANES), F32),
            pltpu.VMEM((SIDE, 32, LANES), F32),
            pltpu.VMEM((SIDE * SIDE, 16, LANES), BF16),
            pltpu.VMEM((4, 8, LANES), F32),
            pltpu.VMEM((2 * SIDE, 8, LANES), F32),
            pltpu.SemaphoreType.DMA((7,)),
            pltpu.SemaphoreType.DMA((10,)),
            pltpu.SemaphoreType.DMA((10,)),
        ],
        compiler_params=pltpu.CompilerParams(
            collective_id=0, has_side_effects=True, vmem_limit_bytes=60 * 1024 * 1024
        ),
    )(queries, keys, values, positions, falloff.reshape(1, 1), ids, cotangent)


def solution(mesh):
    return jax.shard_map(
        shards,
        mesh=mesh,
        in_specs=(
            P(None, "head"),
            P("head", "ctx"),
            P("head", "ctx"),
            P(None, "ctx"),
            P("head"),
            P(),
            P(None, "head"),
        ),
        out_specs=(P("head", None), P("head", None), P()),
        check_vma=False,
    )
```

time: 67.5 us -> 53.5 us (0.79)
  Pallas kernels: 58.9 us -> 49 us
  local copies, waits for them, and re-layouts: 6.98 us -> 2.94 us
    pallas_call x1, Pallas kernels: 58.9 us -> 49 us  [shards(): pl.pallas_call(kernel, out_shape=(jax.ShapeDtypeStruct((HEAD_DIM, nq), BF...]
    unnamed x15 -> x7, local copies, waits for them, and re-layouts: 6.98 us -> 2.94 us
where the time goes in v2:
time: 53.5 us; the launch traced here: 53.3 us
  Pallas kernels  49 us (92%)
  local copies, waits for them, and re-layouts  2.94 us (5%)
  between operations  1.3 us (2%)
    pallas_call x1, Pallas kernels, shards(): pl.pallas_call(kernel, out_shape=(jax.ShapeDtypeStruct((HEAD_DIM, nq), BF...  49 us
    unnamed x7, local copies, waits for them, and re-layouts  2.94 us

profile of v2, /device:TPU:1, one launch (start us, length us, event | category | flops | bytes accessed | tf_op | source)
XLA Modules:
  0.0 53.3 jit_solution(13915462619853322299)
XLA Ops:
  1.3 49.0 %shard_map.94 = (bf16[64,1024]{1,0:T(8,128)(2,1)}, f32[64,1024]{1,0:T(8,128)}, f32[3,1024]{1,0:T(4,128)}) custom-call(bf16[512,128]{1,0:T(8,128)(2,1)} %q_hbm.1, bf16[64,1024]{1,0:T(8,128)(2,1)} %k_hbm.1, bf16[64,1024]{1,0:T(8,128)(2,1)} %v_hbm.1, f32[3,1024]{1,0:T(4,128)} %pos_hbm.1, f32[1,1]{1,0:T(1,128)} %bitcast.2.fall_hbm, s32[8,128]{1,0:T(8,128)} %bitcast.3, ...), custom_call_target="tpu_custom_call" | custom-call | tf_op jit(solution)/shard_map/pallas_call | solution.py:338
  50.3 0.0 copy-start
  50.3 1.6 %copy.14 = bf16[64,1024]{1,0:T(8,128)(2,1)} copy(bf16[64,1024]{1,0:T(8,128)(2,1)} %get-tuple-element.6) | data formatting | bytes 262144
  51.9 0.0 copy-done
  51.9 0.0 copy-start.1
  51.9 0.7 %copy.15 = f32[64,1024]{1,0:T(8,128)} copy(f32[64,1024]{1,0:T(8,128)S(1)} %copy-done) | data formatting | bytes 524288
  52.6 0.0 copy-done.1
  52.7 0.6 %copy.16 = f32[3,1024]{1,0:T(4,128)} copy(f32[3,1024]{1,0:T(4,128)S(1)} %copy-done.1) | data formatting | bytes 24576
Async XLA Ops:
  50.3 1.6 %copy-start = (f32[64,1024]{1,0:T(8,128)S(1)}, f32[64,1024]{1,0:T(8,128)}, u32[]{:S(2)}) copy-start(f32[64,1024]{1,0:T(8,128)} %get-tuple-element.7) | copy-start | bytes 786436
  51.9 0.7 %copy-start.1 = (f32[3,1024]{1,0:T(4,128)S(1)}, f32[3,1024]{1,0:T(4,128)}, u32[]{:S(2)}) copy-start(f32[3,1024]{1,0:T(4,128)} %get-tuple-element.8) | copy-start | bytes 36868

commit v3 on v2

v3 whole, which is shorter than its diff:
```python
import functools

import jax
import jax.numpy as jnp
from jax import lax
from jax.experimental import pallas as pl
from jax.experimental.pallas import tpu as pltpu
from jax.sharding import PartitionSpec as P

MESH = pl.DeviceIdType.MESH
HEAD_DIM = 64
SIDE = 8
LANES = 128
CENTER = 2.0
F32 = jnp.float32
BF16 = jnp.bfloat16


def dot(a, b):
    return jnp.dot(a, b, preferred_element_type=F32)


def pieces(x, count):
    out = []
    for _ in range(count):
        part = x.astype(BF16).astype(F32)
        out.append(part)
        x = x - part
    return out


def rows(shape):
    return lax.broadcasted_iota(jnp.int32, shape, 0)


def total_of(terms):
    return functools.reduce(jnp.add, terms)


def weigh(stats):
    logs = [s[3:4] for s in stats]
    deltas = [s[7:8] for s in stats]
    top = functools.reduce(jnp.maximum, logs)
    weights = [jnp.exp(x - top) for x in logs]
    total = total_of(weights)
    inverse = 1.0 / total
    weights = [w * inverse for w in weights]
    delta = total_of([w * d for w, d in zip(weights, deltas)])
    shifts = [w * (d - delta) for w, d in zip(weights, deltas)]
    plain = total_of([w * s for w, s in zip(weights, stats)])
    moved = total_of([t * pltpu.roll(s, 4, 0) for t, s in zip(shifts, stats)])
    at = rows(plain.shape)
    stat = jnp.where(
        at < 3,
        plain + moved,
        jnp.where(at == 3, top + jnp.log(total), jnp.where(at < 7, plain, delta)),
    )
    return weights, shifts, stat


def combine(weights, shifts, parts):
    a = b = c = None
    for i, (w, t) in enumerate(zip(weights, shifts)):
        ai, bi, ci = parts(i)
        ai, bi, ci = w * ai, w * bi + t * ci, w * ci
        a, b, c = (ai, bi, ci) if a is None else (a + ai, b + bi, c + ci)
    return a, b, c


def kernel(
    q_hbm, k_hbm, v_hbm, pos_hbm, fall_hbm, ids_hbm, g_hbm,
    att_ref, qg_ref, f_ref,
    pos, pos2, fall, ids, left, kt, vt, xs, qin, gin, qx, pick1, sums, pick2, pick3, s_buf, p_buf,
    dp_buf, part_buf, stat_buf, stat2, sb2, rb2, gath, fin, fgath,
    local_sem, send, recv,
):
    h, ctx = lax.axis_index("head"), lax.axis_index("ctx")
    parity = h % 2
    mate = h + 1 - 2 * parity
    y, z = ctx // SIDE, ctx % SIDE
    m1, m2 = SIDE - (SIDE - 1) * parity, 1 + (SIDE - 1) * parity
    a1 = y + parity * (z - y)
    a2 = z + parity * (y - z)

    side = a1 % 2

    def on1(o):
        return ((a1 + o) % SIDE) * m1 + a2 * m2

    def on2(o):
        return a1 * m1 + ((a2 + o) % SIDE) * m2

    def far(k):
        return (SIDE // 2 + (1 - 2 * (k % 2)) * ((k + 1) // 2)) % SIDE

    def copy(phase, src, dst, dev):
        return pltpu.make_async_remote_copy(
            src_ref=src, dst_ref=dst, send_sem=send.at[phase],
            recv_sem=recv.at[phase], device_id=dev, device_id_type=MESH,
        )

    def loop(count, body):
        def step(o, carry):
            body(o)
            return carry
        lax.fori_loop(0, count, step, 0)

    def arrived(phase, ref):
        copy(phase, ref, ref, (h, ctx)).wait_recv()

    def sent(phase, ref):
        copy(phase, ref, ref, (h, ctx)).wait_send()

    def seven(ref):
        return ref.at[pl.ds(0, SIDE - 1)]

    key_count = k_hbm.shape[1]
    own_keys = pl.ds(0, key_count)
    other_keys = pl.ds(key_count, key_count)
    own_rows = pl.ds(pl.multiple_of(h * HEAD_DIM, HEAD_DIM), HEAD_DIM)
    loads = [
        pltpu.make_async_copy(src, dst, local_sem.at[i])
        for i, (src, dst) in enumerate([
            (pos_hbm, pos), (fall_hbm, fall), (ids_hbm, ids),
            (k_hbm, left.at[pl.ds(64, 64), own_keys]), (v_hbm, left.at[pl.ds(0, 64), own_keys]),
            (g_hbm.at[own_rows], gin.at[h]), (q_hbm.at[own_rows], qin.at[h]),
        ])
    ]
    for load in loads[:3]:
        load.start()

    barrier = pltpu.get_barrier_semaphore()

    def greet(head, at):
        pl.semaphore_signal(barrier, inc=1, device_id=(head, at), device_id_type=MESH)

    def greet_seven(k):
        o = far(k)
        greet(h, on1(o))
        greet(h, on2(o))
        greet((h + o) % SIDE, ctx)

    loop(SIDE - 1, greet_seven)
    loop(SIDE, lambda k: greet(mate, on1(far(k))))

    for load in loads[3:]:
        load.start()
    for load in loads[:3]:
        load.wait()
    falloff = fall[...]

    def key_side(ref, cols):
        place = ref[...] - CENTER
        xs[0:3, cols] = place
        xs[3:4, cols] = -falloff * jnp.sum(place * place, axis=0, keepdims=True)
        xs[4:7, cols] = place
        xs[7:8, cols] = jnp.ones((1, key_count), F32)
        x1, x2, x3 = pieces(xs[:, cols], 3)
        left[128:144, cols] = jnp.concatenate([x1, x2], axis=0).astype(BF16)
        return jnp.concatenate([x1, x2, x3, x1], axis=0).astype(BF16)

    keys_at = key_side(pos, own_keys)
    tiles = []
    for i in range(4):
        local = ids[pl.ds(4 * parity + i, 1), :] - ctx * key_count
        hot = (rows((key_count, LANES)) == local).astype(F32).astype(BF16)
        found = dot(keys_at[0:24], hot)
        tiles.append(found[0:8] + found[8:16] + found[16:24])
    low = rows(tiles[0].shape) < 4
    for i in range(2):
        pick1[a1, i] = jnp.where(low, tiles[i], tiles[i + 2])
    pl.semaphore_wait(barrier, 3 * (SIDE - 1) + SIDE)
    loop(SIDE - 1, lambda k: copy(0, pick1.at[a1], pick1.at[a1], (h, on1(far(k)))).start())

    def send_rows(ref_hbm, ref, phase):
        def body(k):
            other = (h + far(k)) % SIDE
            part = pl.ds(pl.multiple_of(other * HEAD_DIM, HEAD_DIM), HEAD_DIM)
            copy(phase, ref_hbm.at[part], ref.at[h], (other, ctx)).start()
        loop(SIDE - 1, body)

    partner = (h, (a1 + 1 - 2 * side) * m1 + a2 * m2)
    share_v = copy(12, v_hbm, left.at[pl.ds(0, 64), other_keys], partner)
    share_k = copy(13, k_hbm, left.at[pl.ds(64, 64), other_keys], partner)
    share_pos = copy(14, pos_hbm, pos2, partner)
    share_pos.start()
    share_v.start()
    share_k.start()
    send_rows(g_hbm, gin, 1)
    send_rows(q_hbm, qin, 2)
    for load in loads[3:]:
        load.wait()

    def turn(cols, at):
        kt[cols, :] = jnp.concatenate([left[64:128, cols], at], axis=0).T
        vt[cols, :] = left[0:64, cols].T

    turn(own_keys, keys_at)
    arrived(0, seven(pick1))
    for i in range(2):
        sums[i] = functools.reduce(jnp.add, [pick1[j, i] for j in range(SIDE)])
    slot2 = SIDE * parity + a2
    pick2[slot2] = sums[side]
    spread = pick2.at[slot2]
    loop(SIDE - 1, lambda k: copy(3, sums.at[side], spread, (h, on2(far(k)))).start())

    def send_mate(k):
        b = (a2 + far(k)) % SIDE
        copy(3, sums.at[b % 2], spread, (mate, a1 * m1 + b * m2)).start()

    loop(SIDE, send_mate)
    arrived(14, pos2)
    arrived(12, left.at[pl.ds(0, 64), other_keys])
    arrived(13, left.at[pl.ds(64, 64), other_keys])
    turn(other_keys, key_side(pos2, other_keys))
    arrived(1, seven(gin))

    def offsets(t):
        return [4 + 2 * t, 2 - 2 * t]

    def chunks(t):
        return [(a1 + o) % SIDE for o in offsets(t)]

    def grads(t):
        cot = jnp.concatenate([gin[c] for c in chunks(t)], axis=1)
        dp_buf[t] = dot(vt[...], cot)

    loop(2, grads)
    arrived(2, seven(qin))
    arrived(3, pick2.at[pl.ds(0, 2 * SIDE - 1)])
    for p in range(2):
        pair = functools.reduce(jnp.add, [pick2[SIDE * p + i] for i in range(SIDE)])
        low = rows(pair.shape) < 4
        swapped = pltpu.roll(pair, 4, 0)
        pick3[2 * p] = jnp.where(low, pair, swapped)
        pick3[2 * p + 1] = jnp.where(low, swapped, pair)

    def build(i):
        spot = pick3[i]
        at = rows(spot.shape)
        t = jnp.where(at < 3, (2.0 * falloff) * spot, jnp.where(at == 3, 1.0, 0.0))
        t1, t2 = pieces(t, 2)
        qx[i, 0:64, :] = qin[2 * i + side] * jnp.asarray(HEAD_DIM ** -0.5, BF16)
        qx[i, 64:96, :] = jnp.concatenate([t1, t1, t1, t2], axis=0).astype(BF16)

    loop(SIDE // 2, build)

    blocks = [pl.ds(i * 256, 256) for i in range(2 * key_count // 256)]

    place1 = a1 // 2
    three = pl.ds(0, 3)

    def attend(t):
        mine = chunks(t)
        q = jnp.concatenate([qx[c // 2] for c in mine], axis=1)
        cot = jnp.concatenate([gin[c] for c in mine], axis=1).astype(F32)
        top = None
        for part in blocks:
            s = dot(kt[part, :], q)
            s_buf[part, :] = s
            m = jnp.max(s, axis=0, keepdims=True)
            top = m if top is None else jnp.maximum(top, m)
        for part in blocks:
            p = jnp.exp(s_buf[part, :] - top)
            s_buf[part, :] = p
            p_buf[part, :] = p.astype(BF16)
        r = dot(left[...], p_buf[...])
        total = r[135:136]
        inverse = 1.0 / total
        a = r[0:64] * inverse
        c = r[64:128] * inverse
        px = (r[128:136] + r[136:144]) * inverse
        delta = jnp.sum(a * cot, axis=0, keepdims=True)
        places = []
        for i in range(2):
            o = offsets(t)[i]
            slot = jnp.where(o == 0, place1, SIDE // 2 + o // 2)
            lanes = slice(i * LANES, (i + 1) * LANES)
            places.append((o, slot, lanes))
            part_buf[slot, 0:64, :] = a[:, lanes].astype(BF16)
            part_buf[slot, 64:128, :] = c[:, lanes].astype(BF16)
            first = pl.ds(0, 128)

            @pl.when(o != 0)
            def _():
                copy(4, part_buf.at[slot, first], part_buf.at[place1, first], (h, on1(o))).start()

        for part in blocks:
            w = s_buf[part, :] * (dp_buf[t, part, :] - delta)
            p_buf[part, :] = w.astype(BF16)
        r = dot(left[64:144, :], p_buf[...])
        b = r[0:64] * inverse
        wx = (r[64:72] + r[72:80]) * inverse
        spot = jnp.concatenate([pick3[c // 2] for c in mine], axis=1)
        at = rows(spot.shape)
        stat = jnp.where(
            at < 3,
            wx - spot * wx[7:8],
            jnp.where(
                at == 3,
                top + jnp.log(total),
                jnp.where(at < 7, px - spot * px[7:8], delta),
            ),
        )
        for o, slot, lanes in places:
            stat_buf[slot] = stat[:, lanes]
            part_buf[slot, 128:192, :] = b[:, lanes].astype(BF16)
            last = pl.ds(128, 64)

            @pl.when(o != 0)
            def _():
                copy(5, stat_buf.at[slot], stat_buf.at[place1], (h, on1(o))).start()
                copy(10, part_buf.at[slot, last], part_buf.at[place1, last], (h, on1(o))).start()

    loop(2, attend)
    arrived(5, stat_buf.at[three])
    weights, shifts, stat = weigh([stat_buf[i] for i in range(SIDE // 2)])
    stat2[a2] = stat
    loop(SIDE - 1, lambda k: copy(11, stat2.at[a2], stat2.at[a2], (h, on2(far(k)))).start())
    arrived(4, part_buf.at[three, pl.ds(0, 128)])
    arrived(10, part_buf.at[three, pl.ds(128, 64)])
    def parts1(i):
        x = part_buf[i].astype(F32)
        return x[0:64], x[128:192], x[64:128]

    a, b, c = combine(weights, shifts, parts1)
    for j in range(SIDE):
        part = slice(8 * j, 8 * j + 8)
        sb2[j] = jnp.concatenate([a[part], b[part], c[part], c[part]], axis=0).astype(BF16)
    def send_second(k):
        o = far(k)
        copy(6, sb2.at[(a2 + o) % SIDE], rb2.at[a2], (h, on2(o))).start()

    loop(SIDE - 1, send_second)
    rb2[a2] = sb2[a2]
    arrived(11, seven(stat2))
    weights, shifts, stat = weigh([stat2[i] for i in range(SIDE)])
    fin[h // 2] = (2.0 * falloff) * stat

    def send_force(k):
        other = (h + 2 + 2 * k) % SIDE
        copy(7, fin.at[h // 2], fin.at[h // 2], (other, ctx)).start()

    loop(3, send_force)
    arrived(6, seven(rb2))
    def parts2(i):
        x = rb2[i].astype(F32)
        return x[0:8], x[8:16], x[16:24]

    a, b, c = combine(weights, shifts, parts2)
    tile = SIDE * a1 + a2
    gath[tile] = jnp.concatenate([a, b * HEAD_DIM ** -0.5], axis=0).astype(BF16)
    def send_tile(k):
        at = ((y + far(k % SIDE)) % SIDE) * SIDE + k // SIDE

        @pl.when(at != ctx)
        def _():
            copy(8, gath.at[tile], gath.at[tile], (h, at)).start()

    loop(SIDE * SIDE // 2, send_tile)
    arrived(7, fin.at[pl.ds(0, 3)])
    fgath[SIDE * parity + a1] = functools.reduce(jnp.add, [fin[i] for i in range(4)])
    ours = fgath.at[SIDE * parity + a1]
    loop(SIDE - 1, lambda k: copy(9, ours, ours, (h, on1(far(k)))).start())
    loop(SIDE, lambda k: copy(9, ours, ours, (mate, on1(far(k)))).start())
    loop(SIDE * SIDE // 2, lambda k: send_tile(k + SIDE * SIDE // 2))
    arrived(8, gath.at[pl.ds(0, SIDE * SIDE - 1)])
    for i in range(SIDE):
        lanes = slice(i * LANES, (i + 1) * LANES)
        for j in range(0, SIDE, 2):
            lo, hi = gath[SIDE * i + j].astype(F32), gath[SIDE * i + j + 1].astype(F32)
            att_ref[8 * j:8 * j + 16, lanes] = jnp.concatenate([lo[0:8], hi[0:8]], axis=0).astype(BF16)
            qg_ref[8 * j:8 * j + 8, lanes] = lo[8:16]
            qg_ref[8 * j + 8:8 * j + 16, lanes] = hi[8:16]
    arrived(9, fgath.at[pl.ds(0, 2 * SIDE - 1)])
    for i in range(SIDE):
        f_ref[:, i * LANES:(i + 1) * LANES] = fgath[i, 0:3, :] + fgath[SIDE + i, 0:3, :]
    sent(0, seven(pick1))
    sent(1, seven(gin))
    sent(2, seven(qin))
    sent(3, pick2.at[pl.ds(0, 2 * SIDE - 1)])
    sent(4, part_buf.at[three, pl.ds(0, 128)])
    sent(10, part_buf.at[three, pl.ds(128, 64)])
    sent(11, seven(stat2))
    sent(12, v_hbm)
    sent(13, k_hbm)
    sent(14, pos2)
    sent(5, stat_buf.at[three])
    sent(6, seven(rb2))
    sent(7, fin.at[pl.ds(0, 3)])
    sent(8, gath.at[pl.ds(0, SIDE * SIDE - 1)])
    sent(9, fgath.at[pl.ds(0, 2 * SIDE - 1)])


def shards(queries, keys, values, positions, falloff, query_ids, cotangent):
    nk = keys.shape[1]
    nq = query_ids.shape[0]
    ids = query_ids.reshape(SIDE, LANES)
    vmem = pl.BlockSpec(memory_space=pltpu.VMEM)
    any_ = pl.BlockSpec(memory_space=pl.ANY)
    return pl.pallas_call(
        kernel,
        out_shape=(
            pltpu.VMEM((HEAD_DIM, nq), BF16),
            pltpu.VMEM((HEAD_DIM, nq), F32),
            pltpu.VMEM((3, nq), F32),
        ),
        in_specs=[any_] * 7,
        out_specs=(vmem, vmem, vmem),
        scratch_shapes=[
            pltpu.VMEM((3, nk), F32),
            pltpu.VMEM((3, nk), F32),
            pltpu.VMEM((1, 1), F32),
            pltpu.VMEM((SIDE, LANES), jnp.int32),
            pltpu.VMEM((144, 2 * nk), BF16),
            pltpu.VMEM((2 * nk, 96), BF16),
            pltpu.VMEM((2 * nk, 64), BF16),
            pltpu.VMEM((8, 2 * nk), F32),
            pltpu.VMEM((SIDE, HEAD_DIM, LANES), BF16),
            pltpu.VMEM((SIDE, HEAD_DIM, LANES), BF16),
            pltpu.VMEM((SIDE // 2, 96, LANES), BF16),
            pltpu.VMEM((SIDE, 2, 8, LANES), F32),
            pltpu.VMEM((2, 8, LANES), F32),
            pltpu.VMEM((2 * SIDE, 8, LANES), F32),
            pltpu.VMEM((SIDE // 2, 8, LANES), F32),
            pltpu.VMEM((2 * nk, 2 * LANES), F32),
            pltpu.VMEM((2 * nk, 2 * LANES), BF16),
            pltpu.VMEM((SIDE // 4, 2 * nk, 2 * LANES), F32),
            pltpu.VMEM((SIDE, 192, LANES), BF16),
            pltpu.VMEM((SIDE, 8, LANES), F32),
            pltpu.VMEM((SIDE, 8, LANES), F32),
            pltpu.VMEM((SIDE, 32, LANES), BF16),
            pltpu.VMEM((SIDE, 32, LANES), BF16),
            pltpu.VMEM((SIDE * SIDE, 16, LANES), BF16),
            pltpu.VMEM((4, 8, LANES), F32),
            pltpu.VMEM((2 * SIDE, 8, LANES), F32),
            pltpu.SemaphoreType.DMA((7,)),
            pltpu.SemaphoreType.DMA((15,)),
            pltpu.SemaphoreType.DMA((15,)),
        ],
        compiler_params=pltpu.CompilerParams(
            collective_id=0, has_side_effects=True, vmem_limit_bytes=56 * 1024 * 1024
        ),
    )(queries, keys, values, positions, falloff.reshape(1, 1), ids, cotangent)


def solution(mesh):
    return jax.shard_map(
        shards,
        mesh=mesh,
        in_specs=(
            P(None, "head"),
            P("head", "ctx"),
            P("head", "ctx"),
            P(None, "ctx"),
            P("head"),
            P(),
            P(None, "head"),
        ),
        out_specs=(P("head", None), P("head", None), P()),
        check_vma=False,
    )
```

time: 53.5 us -> 49.1 us (0.918)
  Pallas kernels: 49 us -> 45.7 us
  local copies, waits for them, and re-layouts: 2.94 us -> 1.96 us
    pallas_call x1, Pallas kernels: 49 us -> 45.7 us  [shards(): pl.pallas_call(kernel, out_shape=(pltpu.VMEM((HEAD_DIM, nq), BF16), pltpu...]
    unnamed x7 -> x3, local copies, waits for them, and re-layouts: 2.94 us -> 1.96 us
where the time goes in v3:
time: 49.1 us; the launch traced here: 48.9 us
  Pallas kernels  45.7 us (93%)
  local copies, waits for them, and re-layouts  1.96 us (4%)
  between operations  1.29 us (3%)
    pallas_call x1, Pallas kernels, shards(): pl.pallas_call(kernel, out_shape=(pltpu.VMEM((HEAD_DIM, nq), BF16), pltpu...  45.7 us
    unnamed x3, local copies, waits for them, and re-layouts  1.96 us

profile of v3, /device:TPU:1, one launch (start us, length us, event | category | flops | bytes accessed | tf_op | source)
XLA Modules:
  0.0 48.9 jit_solution(13566544530247719625)
XLA Ops:
  1.3 45.7 %shard_map.94 = (bf16[64,1024]{1,0:T(8,128)(2,1)S(1)}, f32[64,1024]{1,0:T(8,128)S(1)}, f32[3,1024]{1,0:T(4,128)S(1)}) custom-call(bf16[512,128]{1,0:T(8,128)(2,1)} %q_hbm.1, bf16[64,1024]{1,0:T(8,128)(2,1)} %k_hbm.1, bf16[64,1024]{1,0:T(8,128)(2,1)} %v_hbm.1, f32[3,1024]{1,0:T(4,128)} %pos_hbm.1, f32[1,1]{1,0:T(1,128)} %bitcast.2.fall_hbm, ...), custom_call_target="tpu_custom_call" | custom-call | tf_op jit(solution)/shard_map/pallas_call | solution.py:401
  47.0 0.7 %copy.13 = bf16[64,1024]{1,0:T(8,128)(2,1)} copy(bf16[64,1024]{1,0:T(8,128)(2,1)S(1)} %get-tuple-element.3) | data formatting | bytes 262144
  47.6 0.6 %copy.15 = f32[3,1024]{1,0:T(4,128)} copy(f32[3,1024]{1,0:T(4,128)S(1)} %get-tuple-element.5) | data formatting | bytes 24576
  48.2 0.7 %copy.14 = f32[64,1024]{1,0:T(8,128)} copy(f32[64,1024]{1,0:T(8,128)S(1)} %get-tuple-element.4) | data formatting | bytes 524288

commit v4 on v3

--- a/solution.py
+++ b/solution.py
@@ -392,13 +392,22 @@
     sent(9, fgath.at[pl.ds(0, 2 * SIDE - 1)])
 
 
+def store(*refs):
+    sems = refs[6]
+    copies = [pltpu.make_async_copy(refs[i], refs[3 + i], sems.at[i]) for i in range(3)]
+    for c in copies:
+        c.start()
+    for c in copies:
+        c.wait()
+
+
 def shards(queries, keys, values, positions, falloff, query_ids, cotangent):
     nk = keys.shape[1]
     nq = query_ids.shape[0]
     ids = query_ids.reshape(SIDE, LANES)
     vmem = pl.BlockSpec(memory_space=pltpu.VMEM)
     any_ = pl.BlockSpec(memory_space=pl.ANY)
-    return pl.pallas_call(
+    results = pl.pallas_call(
         kernel,
         out_shape=(
             pltpu.VMEM((HEAD_DIM, nq), BF16),
@@ -442,6 +451,14 @@
             collective_id=0, has_side_effects=True, vmem_limit_bytes=56 * 1024 * 1024
         ),
     )(queries, keys, values, positions, falloff.reshape(1, 1), ids, cotangent)
+    return pl.pallas_call(
+        store,
+        out_shape=tuple(jax.ShapeDtypeStruct(x.shape, x.dtype) for x in results),
+        in_specs=[any_] * 3,
+        out_specs=(any_, any_, any_),
+        scratch_shapes=[pltpu.SemaphoreType.DMA((3,))],
+        compiler_params=pltpu.CompilerParams(vmem_limit_bytes=8 * 1024 * 1024),
+    )(*results)
 
 
 def solution(mesh):

time: 49.1 us -> 47.9 us (0.976)
  local copies, waits for them, and re-layouts: 1.96 us -> 0 us
  Pallas kernels: 45.7 us -> 46.4 us
    unnamed x3 -> x0, local copies, waits for them, and re-layouts: 1.96 us -> none
    pallas_call x0 -> x1, Pallas kernels: none -> 0.78 us  [shards(): pl.pallas_call(store, out_shape=tuple((jax.ShapeDtypeStruct(x.shape, x.dt...]
where the time goes in v4:
time: 47.9 us; the launch traced here: 47.7 us
  Pallas kernels  46.4 us (97%)
  between operations  1.29 us (3%)
    pallas_call x1, Pallas kernels, shards(): pl.pallas_call(kernel, out_shape=(pltpu.VMEM((HEAD_DIM, nq), BF16), pltpu...  45.7 us

profile of v4, /device:TPU:1, one launch (start us, length us, event | category | flops | bytes accessed | tf_op | source)
XLA Modules:
  0.0 47.7 jit_solution(9949016086113048390)
XLA Ops:
  1.3 45.7 %shard_map.94 = (bf16[64,1024]{1,0:T(8,128)(2,1)S(1)}, f32[64,1024]{1,0:T(8,128)S(1)}, f32[3,1024]{1,0:T(4,128)S(1)}) custom-call(bf16[512,128]{1,0:T(8,128)(2,1)} %q_hbm.1, bf16[64,1024]{1,0:T(8,128)(2,1)} %k_hbm.1, bf16[64,1024]{1,0:T(8,128)(2,1)} %v_hbm.1, f32[3,1024]{1,0:T(4,128)} %pos_hbm.1, f32[1,1]{1,0:T(1,128)} %bitcast.2.fall_hbm, ...), custom_call_target="tpu_custom_call" | custom-call | tf_op jit(solution)/shard_map/pallas_call | solution.py:410
  47.0 0.8 %shard_map.95 = (bf16[64,1024]{1,0:T(8,128)(2,1)}, f32[64,1024]{1,0:T(8,128)}, f32[3,1024]{1,0:T(4,128)}) custom-call(bf16[64,1024]{1,0:T(8,128)(2,1)S(1)} %get-tuple-element.6.refs_0_, f32[64,1024]{1,0:T(8,128)S(1)} %get-tuple-element.7.refs_1_, f32[3,1024]{1,0:T(4,128)S(1)} %get-tuple-element.8.refs_2_), custom_call_target="tpu_custom_call" | custom-call | tf_op jit(solution)/shard_map/pallas_call | solution.py:454

commit v5 on v4

--- a/solution.py
+++ b/solution.py
@@ -71,7 +71,7 @@
     q_hbm, k_hbm, v_hbm, pos_hbm, fall_hbm, ids_hbm, g_hbm,
     att_ref, qg_ref, f_ref,
     pos, pos2, fall, ids, left, kt, vt, xs, qin, gin, qx, pick1, sums, pick2, pick3, s_buf, p_buf,
-    dp_buf, part_buf, stat_buf, stat2, sb2, rb2, gath, fin, fgath,
+    dp_buf, part_buf, stat_buf, stat2, sb2, rb2, gath, fgath,
     local_sem, send, recv,
 ):
     h, ctx = lax.axis_index("head"), lax.axis_index("ctx")
@@ -82,7 +82,8 @@
     a1 = y + parity * (z - y)
     a2 = z + parity * (y - z)
 
-    side = a1 % 2
+    side, place1 = a1 % 2, a1 // 2
+    three = pl.ds(0, 3)
 
     def on1(o):
         return ((a1 + o) % SIDE) * m1 + a2 * m2
@@ -246,9 +247,6 @@
     loop(SIDE // 2, build)
 
     blocks = [pl.ds(i * 256, 256) for i in range(2 * key_count // 256)]
-
-    place1 = a1 // 2
-    three = pl.ds(0, 3)
 
     def attend(t):
         mine = chunks(t)
@@ -295,11 +293,11 @@
         at = rows(spot.shape)
         stat = jnp.where(
             at < 3,
-            wx - spot * wx[7:8],
+            (2.0 * falloff) * (wx - spot * wx[7:8]),
             jnp.where(
                 at == 3,
                 top + jnp.log(total),
-                jnp.where(at < 7, px - spot * px[7:8], delta),
+                jnp.where(at < 7, (2.0 * falloff) * (px - spot * px[7:8]), delta),
             ),
         )
         for o, slot, lanes in places:
@@ -315,8 +313,15 @@
     loop(2, attend)
     arrived(5, stat_buf.at[three])
     weights, shifts, stat = weigh([stat_buf[i] for i in range(SIDE // 2)])
-    stat2[a2] = stat
-    loop(SIDE - 1, lambda k: copy(11, stat2.at[a2], stat2.at[a2], (h, on2(far(k)))).start())
+    own = SIDE * (h // 2) + a2
+    stat2[own] = stat
+    ours2 = stat2.at[own]
+    loop(SIDE - 1, lambda k: copy(11, ours2, ours2, (h, on2(far(k)))).start())
+
+    def send_others(k):
+        other = (h + 2 + 2 * (k // SIDE)) % SIDE
+        copy(7, ours2, ours2, (other, on2(far(k % SIDE)))).start()
+
     arrived(4, part_buf.at[three, pl.ds(0, 128)])
     arrived(10, part_buf.at[three, pl.ds(128, 64)])
     def parts1(i):
@@ -332,16 +337,10 @@
         copy(6, sb2.at[(a2 + o) % SIDE], rb2.at[a2], (h, on2(o))).start()
 
     loop(SIDE - 1, send_second)
+    loop(3 * SIDE, send_others)
     rb2[a2] = sb2[a2]
     arrived(11, seven(stat2))
-    weights, shifts, stat = weigh([stat2[i] for i in range(SIDE)])
-    fin[h // 2] = (2.0 * falloff) * stat
-
-    def send_force(k):
-        other = (h + 2 + 2 * k) % SIDE
-        copy(7, fin.at[h // 2], fin.at[h // 2], (other, ctx)).start()
-
-    loop(3, send_force)
+    weights, shifts, _ = weigh([stat2[SIDE * (h // 2) + i] for i in range(SIDE)])
     arrived(6, seven(rb2))
     def parts2(i):
         x = rb2[i].astype(F32)
@@ -358,8 +357,10 @@
             copy(8, gath.at[tile], gath.at[tile], (h, at)).start()
 
     loop(SIDE * SIDE // 2, send_tile)
-    arrived(7, fin.at[pl.ds(0, 3)])
-    fgath[SIDE * parity + a1] = functools.reduce(jnp.add, [fin[i] for i in range(4)])
+    arrived(7, stat2.at[pl.ds(0, 3 * SIDE)])
+    fgath[SIDE * parity + a1] = total_of(
+        [weigh([stat2[SIDE * i + j] for j in range(SIDE)])[2] for i in range(4)]
+    )
     ours = fgath.at[SIDE * parity + a1]
     loop(SIDE - 1, lambda k: copy(9, ours, ours, (h, on1(far(k)))).start())
     loop(SIDE, lambda k: copy(9, ours, ours, (mate, on1(far(k)))).start())
@@ -387,7 +388,7 @@
     sent(14, pos2)
     sent(5, stat_buf.at[three])
     sent(6, seven(rb2))
-    sent(7, fin.at[pl.ds(0, 3)])
+    sent(7, stat2.at[pl.ds(0, 3 * SIDE)])
     sent(8, gath.at[pl.ds(0, SIDE * SIDE - 1)])
     sent(9, fgath.at[pl.ds(0, 2 * SIDE - 1)])
 
@@ -437,11 +438,10 @@
             pltpu.VMEM((SIDE // 4, 2 * nk, 2 * LANES), F32),
             pltpu.VMEM((SIDE, 192, LANES), BF16),
             pltpu.VMEM((SIDE, 8, LANES), F32),
-            pltpu.VMEM((SIDE, 8, LANES), F32),
+            pltpu.VMEM((4 * SIDE, 8, LANES), F32),
             pltpu.VMEM((SIDE, 32, LANES), BF16),
             pltpu.VMEM((SIDE, 32, LANES), BF16),
             pltpu.VMEM((SIDE * SIDE, 16, LANES), BF16),
-            pltpu.VMEM((4, 8, LANES), F32),
             pltpu.VMEM((2 * SIDE, 8, LANES), F32),
             pltpu.SemaphoreType.DMA((7,)),
             pltpu.SemaphoreType.DMA((15,)),

time: 47.9 us -> 47.1 us (0.983)
  Pallas kernels: 46.4 us -> 45.6 us
    pallas_call x1, Pallas kernels: 45.7 us -> 44.8 us  [shards(): pl.pallas_call(kernel, out_shape=(pltpu.VMEM((HEAD_DIM, nq), BF16), pltpu...]
where the time goes in v5:
time: 47.1 us; the launch traced here: 46.9 us
  Pallas kernels  45.6 us (97%)
  between operations  1.29 us (3%)
    pallas_call x1, Pallas kernels, shards(): pl.pallas_call(kernel, out_shape=(pltpu.VMEM((HEAD_DIM, nq), BF16), pltpu...  44.8 us

profile of v5, /device:TPU:1, one launch (start us, length us, event | category | flops | bytes accessed | tf_op | source)
XLA Modules:
  0.0 46.9 jit_solution(14302196581124117571)
XLA Ops:
  1.3 44.8 %shard_map.94 = (bf16[64,1024]{1,0:T(8,128)(2,1)S(1)}, f32[64,1024]{1,0:T(8,128)S(1)}, f32[3,1024]{1,0:T(4,128)S(1)}) custom-call(bf16[512,128]{1,0:T(8,128)(2,1)} %q_hbm.1, bf16[64,1024]{1,0:T(8,128)(2,1)} %k_hbm.1, bf16[64,1024]{1,0:T(8,128)(2,1)} %v_hbm.1, f32[3,1024]{1,0:T(4,128)} %pos_hbm.1, f32[1,1]{1,0:T(1,128)} %bitcast.2.fall_hbm, ...), custom_call_target="tpu_custom_call" | custom-call | tf_op jit(solution)/shard_map/pallas_call | solution.py:411
  46.1 0.8 %shard_map.95 = (bf16[64,1024]{1,0:T(8,128)(2,1)}, f32[64,1024]{1,0:T(8,128)}, f32[3,1024]{1,0:T(4,128)}) custom-call(bf16[64,1024]{1,0:T(8,128)(2,1)S(1)} %get-tuple-element.6.refs_0_, f32[64,1024]{1,0:T(8,128)S(1)} %get-tuple-element.7.refs_1_, f32[3,1024]{1,0:T(4,128)S(1)} %get-tuple-element.8.refs_2_), custom_call_target="tpu_custom_call" | custom-call | tf_op jit(solution)/shard_map/pallas_call | solution.py:454

commit v6 on v5

--- a/solution.py
+++ b/solution.py
@@ -173,11 +173,33 @@
     pl.semaphore_wait(barrier, 3 * (SIDE - 1) + SIDE)
     loop(SIDE - 1, lambda k: copy(0, pick1.at[a1], pick1.at[a1], (h, on1(far(k)))).start())
 
+    def uses(other):
+        return (h + y + (other % 2) * (z - y)) % 2 == 0
+
+    def blocks_arrived(phase, ref):
+        @pl.when((h + a1) % 2 == 0)
+        def _():
+            arrived(phase, ref.at[pl.ds(0, SIDE // 2 - 1)])
+
+        @pl.when((h + a1) % 2 != 0)
+        def _():
+            arrived(phase, ref.at[pl.ds(0, SIDE // 2)])
+
+    def blocks_sent(phase, ref):
+        def body(k):
+            @pl.when(uses((h + far(k)) % SIDE))
+            def _():
+                sent(phase, ref.at[0])
+        loop(SIDE - 1, body)
+
     def send_rows(ref_hbm, ref, phase):
         def body(k):
             other = (h + far(k)) % SIDE
             part = pl.ds(pl.multiple_of(other * HEAD_DIM, HEAD_DIM), HEAD_DIM)
-            copy(phase, ref_hbm.at[part], ref.at[h], (other, ctx)).start()
+
+            @pl.when(uses(other))
+            def _():
+                copy(phase, ref_hbm.at[part], ref.at[h], (other, ctx)).start()
         loop(SIDE - 1, body)
 
     partner = (h, (a1 + 1 - 2 * side) * m1 + a2 * m2)
@@ -214,7 +236,7 @@
     arrived(12, left.at[pl.ds(0, 64), other_keys])
     arrived(13, left.at[pl.ds(64, 64), other_keys])
     turn(other_keys, key_side(pos2, other_keys))
-    arrived(1, seven(gin))
+    blocks_arrived(1, gin)
 
     def offsets(t):
         return [4 + 2 * t, 2 - 2 * t]
@@ -227,7 +249,7 @@
         dp_buf[t] = dot(vt[...], cot)
 
     loop(2, grads)
-    arrived(2, seven(qin))
+    blocks_arrived(2, qin)
     arrived(3, pick2.at[pl.ds(0, 2 * SIDE - 1)])
     for p in range(2):
         pair = functools.reduce(jnp.add, [pick2[SIDE * p + i] for i in range(SIDE)])
@@ -377,8 +399,8 @@
     for i in range(SIDE):
         f_ref[:, i * LANES:(i + 1) * LANES] = fgath[i, 0:3, :] + fgath[SIDE + i, 0:3, :]
     sent(0, seven(pick1))
-    sent(1, seven(gin))
-    sent(2, seven(qin))
+    blocks_sent(1, gin)
+    blocks_sent(2, qin)
     sent(3, pick2.at[pl.ds(0, 2 * SIDE - 1)])
     sent(4, part_buf.at[three, pl.ds(0, 128)])
     sent(10, part_buf.at[three, pl.ds(128, 64)])

time: 47.1 us -> 47.3 us (level)
  no operation moved by 1% of the time
where the time goes in v6:
time: 47.3 us; the launch traced here: 46.9 us
  Pallas kernels  45.6 us (96%)
  between operations  1.29 us (3%)
    pallas_call x1, Pallas kernels, shards(): pl.pallas_call(kernel, out_shape=(pltpu.VMEM((HEAD_DIM, nq), BF16), pltpu...  44.8 us

profile of v6, /device:TPU:1, one launch (start us, length us, event | category | flops | bytes accessed | tf_op | source)
XLA Modules:
  0.0 46.9 jit_solution(14246363300047723478)
XLA Ops:
  1.3 44.8 %shard_map.94 = (bf16[64,1024]{1,0:T(8,128)(2,1)S(1)}, f32[64,1024]{1,0:T(8,128)S(1)}, f32[3,1024]{1,0:T(4,128)S(1)}) custom-call(bf16[512,128]{1,0:T(8,128)(2,1)} %q_hbm.1, bf16[64,1024]{1,0:T(8,128)(2,1)} %k_hbm.1, bf16[64,1024]{1,0:T(8,128)(2,1)} %v_hbm.1, f32[3,1024]{1,0:T(4,128)} %pos_hbm.1, f32[1,1]{1,0:T(1,128)} %bitcast.2.fall_hbm, ...), custom_call_target="tpu_custom_call" | custom-call | tf_op jit(solution)/shard_map/pallas_call | solution.py:433
  46.1 0.8 %shard_map.95 = (bf16[64,1024]{1,0:T(8,128)(2,1)}, f32[64,1024]{1,0:T(8,128)}, f32[3,1024]{1,0:T(4,128)}) custom-call(bf16[64,1024]{1,0:T(8,128)(2,1)S(1)} %get-tuple-element.6.refs_0_, f32[64,1024]{1,0:T(8,128)S(1)} %get-tuple-element.7.refs_1_, f32[3,1024]{1,0:T(4,128)S(1)} %get-tuple-element.8.refs_2_), custom_call_target="tpu_custom_call" | custom-call | tf_op jit(solution)/shard_map/pallas_call | solution.py:476
